TPU v7x, 512 devices: a whole 4x8x8 slice. The times are simulated.
512 devices in a mesh: ctx: 16 (over x, y_hi), fsdp: 32 (over z, y_lo, core).
Axes of the slice: x: 4, y: 8 (y_hi: 4, y_lo: 2; y = y_hi * 2 + y_lo), z: 8, core: 2. Of those that a mesh axis runs over, the one named last changes fastest.
Arguments:
- queries: bfloat16 [2048, 12288], P('ctx', 'fsdp'), may hold values from -200 to 200, as said below
- keys: bfloat16 [2048, 12288], P('ctx', 'fsdp'), may hold values from -200 to 200, as said below
- values: bfloat16 [2048, 12288], P('ctx', 'fsdp'), may hold values from -6 to 6
- query_tangent: bfloat16 [2048, 12288], P('ctx', 'fsdp'), may hold values from -6 to 6
- key_tangent: bfloat16 [2048, 12288], P('ctx', 'fsdp'), may hold values from -6 to 6
- value_tangent: bfloat16 [2048, 12288], P('ctx', 'fsdp'), may hold values from -6 to 6
- query_gain: float32 [3072], P('fsdp'), may hold values from 0.5 to 1.5
- key_gain: float32 [3072], P('fsdp'), may hold values from 0.5 to 1.5
- time_index: int32 [4], replicated, may hold values from 0 to 999
- shard_order: int32 [16], P('ctx'), may hold values from 0 to 15, each once
Outputs:
- query_grad: bfloat16 [2048, 12288], P('ctx', 'fsdp')
- key_grad: bfloat16 [2048, 12288], P('ctx', 'fsdp')
- value_grad: bfloat16 [2048, 12288], P('ctx', 'fsdp')
- query_gain_grad: float32 [3072], P('fsdp')
- key_gain_grad: float32 [3072], P('fsdp')
Inputs may be any that keep to these rules, and one draw needn't show every extreme that they name: `queries`: each sample's channels hold 24 heads of 128 channels in order. `keys`: laid out as the queries. `shard_order`: each block index appears once.
All inputs are finite; a program needn't handle non-finite values.
Results may differ from a plain program's by a relative error of at most 0.024.
Values may be sent and summed in bfloat16 or wider, within the bound.
A program may use at most 64 MiB of HBM per device.

v0:
```python
import math

import jax
import jax.numpy as jnp
from jax import lax
from jax.sharding import PartitionSpec as P

HD = 128
HEAD_SPLIT = 8
STEPS = 1000
CHANNELS = 3072


eps_norm = 1e-06
loss_scale = 256.0
rope_base = 10000.0
floor_term = 0.1


def partner_2(value, axis, apart):
    mask = 2**apart
    pairs = [(source, source ^ mask) for source in range(lax.axis_size(axis))]
    return lax.ppermute(value, axis, pairs)


def gather_turned(arrays, axis, dims):
    turned = [jnp.moveaxis(a, dim, 0) for a, dim in zip(arrays, dims)]
    both = jnp.concatenate([t.reshape(len(t), -1) for t in turned], axis=1)
    whole, at, outs = (lax.all_gather(both, axis, axis=0, tiled=True), 0, [])
    for t, dim in zip(turned, dims):
        piece = whole[:, at : at + t[0].size].reshape(-1, *t.shape[1:])
        outs.append(jnp.moveaxis(piece, 0, dim))
        at += t[0].size
    return tuple(outs)


def sent_together(arrays, axis, dim, along):
    ends, at = ([], 0)
    for a in arrays[:-1]:
        at += a.shape[along]
        ends.append(at)
    both = jnp.concatenate(arrays, axis=along)
    return tuple(jnp.split(lax.all_gather(both, axis, axis=dim, tiled=True), ends, axis=along))


def from_everyone(x, axis):
    peers = lax.axis_size(axis)
    return lax.all_to_all(jnp.broadcast_to(x[None], (peers, *x.shape)), axis, 0, 0, tiled=True)


def over_copies(x, axis):
    everything = from_everyone(x, axis)
    return jnp.sum(everything, axis=0)


def packed_total(arrays, axis):
    vector, at, outs = (jnp.concatenate([a.reshape(-1) for a in arrays]), 0, [])
    subtotal = over_copies(vector, axis)
    for a in arrays:
        outs.append(subtotal[at : at + a.size].reshape(a.shape))
        at += a.size
    return tuple(outs)


def split_up(x, dim, peers):
    shape = x.shape
    pieces = x.reshape(*shape[:dim], peers, shape[dim] // peers, *shape[dim + 1 :])
    return jnp.moveaxis(pieces, dim, 0)


def sum_at_owner(x, axis, dim):
    peers = lax.axis_size(axis)
    pieces = lax.all_to_all(split_up(x, dim, peers), axis, 0, 0, tiled=True)
    return jnp.sum(pieces, axis=0)


def group_sum(pieces):
    totals = pieces
    for bit_index in range(HEAD_SPLIT.bit_length() - 1):
        partner = partner_2(totals, "fsdp", bit_index)
        totals = tuple((own_part + far_part for own_part, far_part in zip(totals, partner)))
    return totals


def rotate(field, cos_table, sin_table, turn_sign):
    half_width = field.shape[-1] // 2
    first_half = field[..., :half_width]
    second_half = field[..., half_width:]
    return jnp.concatenate(
        [
            first_half * cos_table - turn_sign * second_half * sin_table,
            turn_sign * first_half * sin_table + second_half * cos_table,
        ],
        axis=-1,
    )


def attend(carry, query_n, query_nt, pieces, head_count):
    key_blk, value_blk, ktan_blk, vtan_blk = tuple(
        (piece.reshape(piece.shape[0], head_count, HD) for piece in pieces)
    )
    peak, totals, numer, numer_tan, tilt = carry
    inv_root = HD ** (-0.5)
    scores = (
        jnp.einsum("thd,khd->thk", query_n, key_blk, preferred_element_type=jnp.float32) * inv_root
    )
    slopes = (
        jnp.einsum("thd,khd->thk", query_nt, key_blk, preferred_element_type=jnp.float32)
        + jnp.einsum("thd,khd->thk", query_n, ktan_blk, preferred_element_type=jnp.float32)
    ) * inv_root
    new_peak = jnp.maximum(peak, jnp.max(scores, axis=-1))
    shrink = jnp.exp(peak - new_peak)
    weights = jnp.exp(scores - new_peak[..., None])
    tilted = weights * slopes
    weights_b = weights.astype(jnp.bfloat16)
    tilted_b = tilted.astype(jnp.bfloat16)
    totals = totals * shrink + jnp.sum(weights, axis=-1)
    numer = numer * shrink[..., None] + jnp.einsum(
        "thk,khd->thd", weights_b, value_blk, preferred_element_type=jnp.float32
    )
    numer_tan = (
        numer_tan * shrink[..., None]
        + jnp.einsum("thk,khd->thd", weights_b, vtan_blk, preferred_element_type=jnp.float32)
        + jnp.einsum("thk,khd->thd", tilted_b, value_blk, preferred_element_type=jnp.float32)
    )
    tilt = tilt * shrink + jnp.sum(tilted, axis=-1)
    return (new_peak, totals, numer, numer_tan, tilt)


def query_side(query_n, cotangent, logsum, drift, key_blk, value_blk):
    inv_root = HD ** (-0.5)
    scores = (
        jnp.einsum("thd,khd->thk", query_n, key_blk, preferred_element_type=jnp.float32) * inv_root
    )
    probs = jnp.exp(scores - logsum[..., None])
    dprobs = jnp.einsum("thd,khd->thk", cotangent, value_blk, preferred_element_type=jnp.float32)
    dscore = (probs * (dprobs - drift[..., None]) * inv_root).astype(jnp.bfloat16)
    return jnp.einsum("thk,khd->thd", dscore, key_blk, preferred_element_type=jnp.float32)


def key_side(query_blk, cot_blk, logsum_blk, drift_blk, key_own, value_own):
    inv_root = HD ** (-0.5)
    scores = (
        jnp.einsum("thd,khd->thk", query_blk, key_own, preferred_element_type=jnp.float32)
        * inv_root
    )
    probs = jnp.exp(scores - logsum_blk[..., None])
    probs_b = probs.astype(jnp.bfloat16)
    dvalue = jnp.einsum("thk,thd->khd", probs_b, cot_blk, preferred_element_type=jnp.float32)
    dprobs = jnp.einsum("thd,khd->thk", cot_blk, value_own, preferred_element_type=jnp.float32)
    dscore = (probs * (dprobs - drift_blk[..., None]) * inv_root).astype(jnp.bfloat16)
    dkey = jnp.einsum("thk,thd->khd", dscore, query_blk, preferred_element_type=jnp.float32)
    return (dkey, dvalue)


def per_device(
    queries,
    keys,
    values,
    query_tangent,
    key_tangent,
    value_tangent,
    query_gain,
    key_gain,
    time_index,
    shard_order,
):
    tok_rows = queries.shape[0]
    ch_dev = queries.shape[1]
    head_count = ch_dev // HD
    rank_in = lax.axis_index("fsdp") % HEAD_SPLIT
    sample_id = lax.axis_index("fsdp") // HEAD_SPLIT
    gains_all = gather_turned((query_gain, key_gain), "fsdp", (0, 0))
    query_gvec = lax.dynamic_slice_in_dim(gains_all[0], rank_in * ch_dev, ch_dev, 0)
    key_gvec = lax.dynamic_slice_in_dim(gains_all[1], rank_in * ch_dev, ch_dev, 0)
    places = (shard_order[0] * tok_rows + jnp.arange(tok_rows, dtype=jnp.int32)).astype(jnp.float32)
    freqs = rope_base ** (-jnp.arange(HD // 2, dtype=jnp.float32) / (HD // 2))
    angles = places[:, None] * freqs[None, :]
    cos_table = jnp.cos(angles)[:, None, :]
    sin_table = jnp.sin(angles)[:, None, :]
    query_x = queries.astype(jnp.float32)
    key_x = keys.astype(jnp.float32)
    query_dx = query_tangent.astype(jnp.float32)
    key_dx = key_tangent.astype(jnp.float32)
    stats = group_sum(
        (
            jnp.sum(query_x * query_x, axis=1),
            jnp.sum(key_x * key_x, axis=1),
            jnp.sum(query_x * query_dx, axis=1),
            jnp.sum(key_x * key_dx, axis=1),
        )
    )
    query_r = lax.rsqrt(stats[0] / CHANNELS + eps_norm)[:, None]
    key_r = lax.rsqrt(stats[1] / CHANNELS + eps_norm)[:, None]
    query_y = query_x * query_r * query_gvec
    key_y = key_x * key_r * key_gvec
    query_yt = (
        query_dx * query_r - query_x * query_r**3 * (stats[2] / CHANNELS)[:, None]
    ) * query_gvec
    key_yt = (key_dx * key_r - key_x * key_r**3 * (stats[3] / CHANNELS)[:, None]) * key_gvec

    def rotated(field):
        return rotate(field.reshape(tok_rows, head_count, HD), cos_table, sin_table, 1.0).astype(
            jnp.bfloat16
        )

    query_n = rotated(query_y)
    query_nt = rotated(query_yt)
    key_flat = rotated(key_y).reshape(tok_rows, ch_dev)
    ktan_flat = rotated(key_yt).reshape(tok_rows, ch_dev)
    zero_rows = jnp.zeros((tok_rows, head_count), jnp.float32)
    zero_field = jnp.zeros((tok_rows, head_count, HD), jnp.float32)
    init_state = (
        jnp.full((tok_rows, head_count), -1e30, jnp.float32),
        zero_rows,
        zero_field,
        zero_field,
        zero_rows,
    )
    gathered = sent_together((key_flat, values, ktan_flat, value_tangent), "ctx", 0, 1)
    seq_rows = gathered[0].shape[0]
    block_rows = math.gcd(seq_rows, 512)

    def scan_step(carry, block_id):
        pieces = tuple(
            (
                lax.dynamic_slice_in_dim(whole, block_id * block_rows, block_rows, 0)
                for whole in gathered
            )
        )
        return (attend(carry, query_n, query_nt, pieces, head_count), None)

    fold_state, unused = lax.scan(
        scan_step, init_state, jnp.arange(seq_rows // block_rows, dtype=jnp.int32)
    )
    peak, totals, numer, numer_tan, tilt = fold_state
    outputs = numer / totals[..., None]
    output_tan = numer_tan / totals[..., None] - (tilt / totals)[..., None] * outputs
    logsum = peak + jnp.log(totals)
    slot_count = time_index.shape[0]
    picked = jnp.sum(jnp.where(jnp.arange(slot_count, dtype=jnp.int32) == sample_id, time_index, 0))
    angle_t = 0.5 * math.pi * (picked.astype(jnp.float32) + 0.5) / STEPS
    raw_target = jnp.sin(angle_t) * jnp.cos(angle_t) * outputs + jnp.cos(angle_t) ** 2 * output_tan
    energy = group_sum((jnp.sum(raw_target * raw_target, axis=(1, 2)),))[0]
    level = jnp.sqrt(energy / CHANNELS)[:, None, None]
    cotangent = (loss_scale * raw_target / (level + floor_term)).astype(jnp.bfloat16)
    drift = jnp.sum(cotangent.astype(jnp.float32) * outputs, axis=-1)
    cycle_size = lax.axis_size("ctx")
    key_own = key_flat.reshape(tok_rows, head_count, HD)
    value_own = values.reshape(tok_rows, head_count, HD)
    stats_all = sent_together((logsum, drift), "ctx", 0, 1)
    pieces = sent_together((query_n, cotangent), "ctx", 0, 1)
    logsum_blk = stats_all[0]
    drift_blk = stats_all[1]
    dkey_add, dvalue_add = key_side(pieces[0], pieces[1], logsum_blk, drift_blk, key_own, value_own)

    def query_step(carry, block_id):
        key_blk = lax.dynamic_slice_in_dim(gathered[0], block_id * tok_rows, tok_rows, 0)
        value_blk = lax.dynamic_slice_in_dim(gathered[1], block_id * tok_rows, tok_rows, 0)
        return (
            carry
            + query_side(
                query_n,
                cotangent,
                logsum,
                drift,
                key_blk.reshape(tok_rows, head_count, HD),
                value_blk.reshape(tok_rows, head_count, HD),
            ),
            None,
        )

    dquery_hat, unused = lax.scan(query_step, zero_field, jnp.arange(cycle_size, dtype=jnp.int32))
    value_grad = dvalue_add.reshape(tok_rows, ch_dev).astype(jnp.bfloat16)
    query_dy = rotate(dquery_hat, cos_table, sin_table, -1.0).reshape(tok_rows, ch_dev)
    key_dy = rotate(dkey_add, cos_table, sin_table, -1.0).reshape(tok_rows, ch_dev)
    query_h = query_gvec * query_dy
    key_h = key_gvec * key_dy
    crosses = group_sum((jnp.sum(query_x * query_h, axis=1), jnp.sum(key_x * key_h, axis=1)))
    query_grad = (
        query_r * query_h - query_x * query_r**3 * (crosses[0] / CHANNELS)[:, None]
    ).astype(jnp.bfloat16)
    key_grad = (key_r * key_h - key_x * key_r**3 * (crosses[1] / CHANNELS)[:, None]).astype(
        jnp.bfloat16
    )
    query_part = jnp.sum(query_dy * query_x * query_r, axis=0)
    key_part = jnp.sum(key_dy * key_x * key_r, axis=0)
    empty_vec = jnp.zeros((CHANNELS,), jnp.float32)
    query_full = lax.dynamic_update_slice_in_dim(empty_vec, query_part, rank_in * ch_dev, 0)
    key_full = lax.dynamic_update_slice_in_dim(empty_vec, key_part, rank_in * ch_dev, 0)
    summed_ctx = packed_total((query_full, key_full), "ctx")
    query_gain_grad, key_gain_grad = (
        sum_at_owner(summed_ctx[0], "fsdp", 0),
        sum_at_owner(summed_ctx[1], "fsdp", 0),
    )
    return (query_grad, key_grad, value_grad, query_gain_grad, key_gain_grad)


def solution(mesh):
    placed = (
        P("ctx", "fsdp"),
        P("ctx", "fsdp"),
        P("ctx", "fsdp"),
        P("ctx", "fsdp"),
        P("ctx", "fsdp"),
        P("ctx", "fsdp"),
        P("fsdp"),
        P("fsdp"),
        P(),
        P("ctx"),
    )
    return jax.shard_map(
        per_device,
        mesh=mesh,
        in_specs=placed,
        out_specs=(P("ctx", "fsdp"), P("ctx", "fsdp"), P("ctx", "fsdp"), P("fsdp"), P("fsdp")),
        check_vma=False,
    )
```

profile of v0, /device:TPU:1, one launch (start us, length us, event | category | flops | bytes accessed | tf_op | source)
XLA Modules:
  0.0 423.8 jit_solution(2000722103080637975)
XLA Ops:
  7.2 1.0 copy.212
  8.2 1.0 copy.226
  9.4 8.8 %collective-permute-start = (f32[128]{0:T(128)S(1)}, f32[128]{0:T(128)S(1)}, u32[]{:S(2)}, u32[]{:S(2)}) collective-permute-start(f32[128]{0:T(128)S(1)} %get-tuple-element.276), channel_id=1, source_target_pairs={{0,1},{1,0},{2,3},{3,2},{4,5},{5,4},{6,7},{7,6},{8,9},{9,8},{10,11... | collective-permute-start | bytes 1544 | tf_op jit(solution)/shard_map/ppermute | solution.py:23
  18.2 1.9 collective-permute-start.9
  20.1 1.0 copy.214
  21.1 1.0 copy.218
  22.2 2.4 collective-permute-start.3
  24.6 1.9 collective-permute-start.6
  27.3 35.4 %all-gather = f32[32,96,2]{1,2,0:T(2,128)S(1)} all-gather(f32[1,96,2]{1,2,0:T(2,128)S(1)} %maximum_bitcast_fusion), channel_id=1, replica_groups=mesh['ctx'=16,'fsdp'=32] {'fsdp'}, dimensions={0}, use_global_device_ids=true | all-gather | bytes 25344 | tf_op jit(solution)/shard_map/all_gather | solution.py:29
  63.5 0.9 broadcast_multiply_fusion
  64.5 1.9 collective-permute-start.1
  66.4 1.0 copy.222
  67.5 3.4 collective-permute-start.10
  70.9 1.9 collective-permute-start.4
  72.8 3.4 collective-permute-start.7
  76.2 1.9 collective-permute-start.2
  78.1 1.0 copy.223
  79.2 3.4 collective-permute-start.11
  82.6 1.9 collective-permute-start.5
  84.5 3.4 collective-permute-start.8
  93.2 106.9 %all-gather.4.cloned.1.call-done = bf16[2048,1536]{0,1:T(8,128)(2,1)} async-done(((bf16[128,1536]{0,1:T(8,128)(2,1)}), bf16[2048,1536]{0,1:T(8,128)(2,1)}) %all-gather.4.cloned.1.call-update) | async-done | bytes 6291472 | tf_op jit(solution)/shard_map/all_gather | solution.py:43
  200.1 5.3 %fusion.68 = (bf16[2048,384]{0,1:T(8,128)(2,1)}, bf16[2048,384]{0,1:T(8,128)(2,1)}, bf16[2048,384]{0,1:T(8,128)(2,1)S(1)}, bf16[2048,384]{0,1:T(8,128)(2,1)}) fusion(bf16[2048,1536]{0,1:T(8,128)(2,1)} %all-gather.4.cloned.1.call-done), kind=kLoop, calls=%fused_computation.147 | loop fusion | bytes 12582912 | tf_op jit(solution)/shard_map/split | solution.py:43
  205.4 25.3 %while.30 = (s32[]{:T(128)}, f32[128,3]{0,1:T(4,128)S(1)}, f32[128,3]{0,1:T(4,128)S(1)}, f32[128,3,128]{0,2,1:T(8,128)S(1)}, f32[128,3,128]{0,2,1:T(8,128)}, /*i...) while((s32[]{:T(128)}, f32[128,3]{0,1:T(4,128)S(1)}, ...), condition=%wide.region_8.9_spmd.clone, body=%wide.region_4.8_spmd.clone.sunk | while | flops 305089152 | bytes 14094785 | solution.py:233
  206.7 1.1 constant_dynamic-slice_fusion.9
  208.4 1.2 constant_dynamic-slice_fusion.10
  213.0 1.1 constant_dynamic-slice_fusion.9
  214.8 1.2 constant_dynamic-slice_fusion.10
  219.3 1.1 constant_dynamic-slice_fusion.9
  221.1 1.2 constant_dynamic-slice_fusion.10
  225.6 1.1 constant_dynamic-slice_fusion.9
  227.4 1.2 constant_dynamic-slice_fusion.10
  230.8 1.1 copy.230
  232.2 2.4 collective-permute-start.12
  235.3 1.9 collective-permute-start.13
  237.3 2.4 collective-permute-done.13
  239.6 1.9 collective-permute-start.14
  241.6 2.3 collective-permute-done.14
  244.2 1.7 pad_maximum_fusion.2
  245.9 45.9 %while.31 = (s32[]{:T(128)}, f32[128,3,128]{0,2,1:T(8,128)S(1)}, s32[16]{0:T(128)S(1)}, bf16[2048,384]{0,1:T(8,128)(2,1)}, bf16[128,3,128]{2,0,1:T(8,128)(2,1)S(...) while((s32[]{:T(128)}, f32[128,3,128]{0,2,1:T(8,128)S(1)}, ...), condition=%wide.region_13.14_spmd.clone, body=%wide.region_12.13_spmd.clone.sunk | while | flops 38141960 | bytes 1576133 | solution.py:273
  261.5 0.9 constant_dynamic-slice_fusion.11
  291.9 37.3 %all_gather.15 = f32[2048,6]{0,1:T(8,128)S(1)} all-gather(f32[128,6]{0,1:T(8,128)S(1)} %pad_maximum_fusion.8), channel_id=1, replica_groups=mesh['ctx'=16,'fsdp'=32] {'ctx'}, dimensions={0}, use_global_device_ids=true | all-gather | bytes 52224 | tf_op jit(solution)/shard_map/all_gather | solution.py:43
  329.9 2.2 fusion.29
  336.3 1.1 copy.240
  338.2 1.8 pad_maximum_fusion.1
  340.0 1.1 copy.233
  341.0 10.8 %collective-permute-start.18 = (f32[128]{0:T(128)}, f32[128]{0:T(128)}, u32[]{:S(2)}, u32[]{:S(2)}) collective-permute-start(f32[128]{0:T(128)} %get-tuple-element.274), channel_id=1, source_target_pairs={{0,1},{1,0},{2,3},{3,2},{4,5},{5,4},{6,7},{7,6},{8,9},{9,8},{10,11... | collective-permute-start | bytes 1544 | tf_op jit(solution)/shard_map/ppermute | solution.py:23
  352.7 1.9 collective-permute-start.15
  357.0 1.2 add.197
  358.2 3.1 collective-permute-start.19
  361.9 1.0 broadcast_in_dim.18
  362.9 4.2 all-to-all-start
  367.1 1.2 add.193
  368.3 2.2 collective-permute-start.16
  370.5 1.2 add.198
  371.7 4.4 %collective-permute-start.20 = (f32[128]{0:T(128)}, f32[128]{0:T(128)}, u32[]{:S(2)}, u32[]{:S(2)}) collective-permute-start(f32[128]{0:T(128)} %add.198), channel_id=1, source_target_pairs={{0,4},{1,5},{2,6},{3,7},{4,0},{5,1},{6,2},{7,3},{8,12},{9,13},{10,... | collective-permute-start | bytes 1544 | tf_op jit(solution)/shard_map/ppermute | solution.py:23
  376.1 3.2 fusion.38
  379.3 1.6 copy.248
  381.6 1.9 collective-permute-start.17
  384.2 1.0 fusion.48
  385.3 1.2 reduce_sum.155
  387.3 9.3 %all-to-all-start.1 = ((f32[32,1,96]{2,1,0:T(1,128)}), f32[32,1,96]{2,1,0:T(1,128)S(1)}, u32[]{:S(2)}, u32[]{:S(2)}) async-start(f32[32,1,96]{2,1,0:T(1,128)} %all_to_all.17), calls=%async_computation.1 | async-start | bytes 32768 | tf_op jit(solution)/shard_map/all_to_all | solution.py:73
  397.3 7.0 %all-to-all-done.1 = f32[32,1,96]{2,1,0:T(1,128)S(1)} async-done(((f32[32,1,96]{2,1,0:T(1,128)}), f32[32,1,96]{2,1,0:T(1,128)S(1)}, u32[]{:S(2)}, u32[]{:S(2)}) %all-to-all-start.1) | async-done | bytes 12320 | tf_op jit(solution)/shard_map/all_to_all | solution.py:73
  404.3 4.1 all-to-all-start.2
  411.3 5.1 %all-to-all-done.2 = f32[32,1,96]{2,1,0:T(1,128)S(1)} async-done(((f32[32,1,96]{2,1,0:T(1,128)}), f32[32,1,96]{2,1,0:T(1,128)S(1)}, u32[]{:S(2)}, u32[]{:S(2)}) %all-to-all-start.2) | async-done | bytes 12320 | tf_op jit(solution)/shard_map/all_to_all | solution.py:73
  (309 shorter events, 69.4 us)
Async XLA Ops:
  7.2 193.0 %all-gather.4.cloned.1.call-start = ((), (), s32[]{:S(2)}) async-start(), calls=%async_computation.3 | async-start | bytes 6684672 | tf_op jit(solution)/shard_map/all_gather | solution.py:43
  8.2 81.5 %copy-start.3 = (bf16[128,384]{0,1:T(8,128)(2,1)}, bf16[128,384]{0,1:T(8,128)(2,1)S(1)}, u32[]{:S(2)}) copy-start(bf16[128,384]{0,1:T(8,128)(2,1)S(1)} %copy.212) | copy-start | bytes 294916
  9.4 55.1 %collective-permute-start = (f32[128]{0:T(128)S(1)}, f32[128]{0:T(128)S(1)}, u32[]{:S(2)}, u32[]{:S(2)}) collective-permute-start(f32[128]{0:T(128)S(1)} %get-tuple-element.276), channel_id=1, source_target_pairs={{0,1},{1,0},{2,3},{3,2},{4,5},{5,4},{6,7},{7,6},{8,9},{9,8},{10,11... | collective-permute-start | bytes 1544 | tf_op jit(solution)/shard_map/ppermute | solution.py:23
  18.2 49.3 %collective-permute-start.9 = (f32[128]{0:T(128)S(1)}, f32[128]{0:T(128)S(1)}, u32[]{:S(2)}, u32[]{:S(2)}) collective-permute-start(f32[128]{0:T(128)S(1)} %get-tuple-element.275), channel_id=1, source_target_pairs={{0,1},{1,0},{2,3},{3,2},{4,5},{5,4},{6,7},{7,6},{8,9},{9,8},{10,11... | collective-permute-start | bytes 1544 | tf_op jit(solution)/shard_map/ppermute | solution.py:23
  21.1 68.7 %copy-start.5 = (bf16[128,384]{0,1:T(8,128)(2,1)}, bf16[128,384]{0,1:T(8,128)(2,1)S(1)}, u32[]{:S(2)}) copy-start(bf16[128,384]{0,1:T(8,128)(2,1)S(1)} %copy.214) | copy-start | bytes 294916
  22.2 48.6 %collective-permute-start.3 = (f32[128]{0:T(128)S(1)}, f32[128]{0:T(128)S(1)}, u32[]{:S(2)}, u32[]{:S(2)}) collective-permute-start(f32[128]{0:T(128)S(1)} %get-tuple-element.277), channel_id=1, source_target_pairs={{0,1},{1,0},{2,3},{3,2},{4,5},{5,4},{6,7},{7,6},{8,9},{9,8},{10,11... | collective-permute-start | bytes 1544 | tf_op jit(solution)/shard_map/ppermute | solution.py:23
  24.6 48.2 %collective-permute-start.6 = (f32[128]{0:T(128)S(1)}, f32[128]{0:T(128)S(1)}, u32[]{:S(2)}, u32[]{:S(2)}) collective-permute-start(f32[128]{0:T(128)S(1)} %get-tuple-element.278), channel_id=1, source_target_pairs={{0,1},{1,0},{2,3},{3,2},{4,5},{5,4},{6,7},{7,6},{8,9},{9,8},{10,11... | collective-permute-start | bytes 1544 | tf_op jit(solution)/shard_map/ppermute | solution.py:23
  64.4 25.9 %copy-start.8 = (f32[128,64]{1,0:T(8,128)}, f32[128,64]{1,0:T(8,128)S(1)}, u32[]{:S(2)}) copy-start(f32[128,64]{1,0:T(8,128)S(1)} %get-tuple-element.387) | copy-start | bytes 98308
  64.4 24.1 %copy-start.19 = (f32[384]{0:T(512)}, f32[384]{0:T(512)S(1)}, u32[]{:S(2)}) copy-start(f32[384]{0:T(512)S(1)} %dynamic-slice_reduce_fusion.1) | copy-start | bytes 4612
  64.5 24.9 %copy-start.21 = (f32[384]{0:T(512)}, f32[384]{0:T(512)S(1)}, u32[]{:S(2)}) copy-start(f32[384]{0:T(512)S(1)} %dynamic-slice_reduce_fusion) | copy-start | bytes 4612
  64.5 11.7 %collective-permute-start.1 = (f32[128]{0:T(128)S(1)}, f32[128]{0:T(128)S(1)}, u32[]{:S(2)}, u32[]{:S(2)}) collective-permute-start(f32[128]{0:T(128)S(1)} %add.162), channel_id=1, source_target_pairs={{0,2},{1,3},{2,0},{3,1},{4,6},{5,7},{6,4},{7,5},{8,10},{9,11},{10,... | collective-permute-start | bytes 1544 | tf_op jit(solution)/shard_map/ppermute | solution.py:23
  67.4 23.2 %copy-start.10 = (bf16[128,384]{0,1:T(8,128)(2,1)}, bf16[128,384]{0,1:T(8,128)(2,1)S(1)}, u32[]{:S(2)}) copy-start(bf16[128,384]{0,1:T(8,128)(2,1)S(1)} %copy.222) | copy-start | bytes 294916
  67.5 11.7 %collective-permute-start.10 = (f32[128]{0:T(128)S(1)}, f32[128]{0:T(128)S(1)}, u32[]{:S(2)}, u32[]{:S(2)}) collective-permute-start(f32[128]{0:T(128)S(1)} %add.180), channel_id=1, source_target_pairs={{0,2},{1,3},{2,0},{3,1},{4,6},{5,7},{6,4},{7,5},{8,10},{9,11},{10,... | collective-permute-start | bytes 1544 | tf_op jit(solution)/shard_map/ppermute | solution.py:23
  70.9 11.7 %collective-permute-start.4 = (f32[128]{0:T(128)S(1)}, f32[128]{0:T(128)S(1)}, u32[]{:S(2)}, u32[]{:S(2)}) collective-permute-start(f32[128]{0:T(128)S(1)} %add.168), channel_id=1, source_target_pairs={{0,2},{1,3},{2,0},{3,1},{4,6},{5,7},{6,4},{7,5},{8,10},{9,11},{10,... | collective-permute-start | bytes 1544 | tf_op jit(solution)/shard_map/ppermute | solution.py:23
  72.8 11.7 %collective-permute-start.7 = (f32[128]{0:T(128)S(1)}, f32[128]{0:T(128)S(1)}, u32[]{:S(2)}, u32[]{:S(2)}) collective-permute-start(f32[128]{0:T(128)S(1)} %add.175), channel_id=1, source_target_pairs={{0,2},{1,3},{2,0},{3,1},{4,6},{5,7},{6,4},{7,5},{8,10},{9,11},{10,... | collective-permute-start | bytes 1544 | tf_op jit(solution)/shard_map/ppermute | solution.py:23
  76.2 11.7 %collective-permute-start.2 = (f32[128]{0:T(128)S(1)}, f32[128]{0:T(128)S(1)}, u32[]{:S(2)}, u32[]{:S(2)}) collective-permute-start(f32[128]{0:T(128)S(1)} %add.163), channel_id=1, source_target_pairs={{0,4},{1,5},{2,6},{3,7},{4,0},{5,1},{6,2},{7,3},{8,12},{9,13},{10,... | collective-permute-start | bytes 1544 | tf_op jit(solution)/shard_map/ppermute | solution.py:23
  79.2 8.8 %collective-permute-start.11 = (f32[128]{0:T(128)S(1)}, f32[128]{0:T(128)S(1)}, u32[]{:S(2)}, u32[]{:S(2)}) collective-permute-start(f32[128]{0:T(128)S(1)} %add.181), channel_id=1, source_target_pairs={{0,4},{1,5},{2,6},{3,7},{4,0},{5,1},{6,2},{7,3},{8,12},{9,13},{10,... | collective-permute-start | bytes 1544 | tf_op jit(solution)/shard_map/ppermute | solution.py:23
  82.6 5.9 %collective-permute-start.5 = (f32[128]{0:T(128)S(1)}, f32[128]{0:T(128)S(1)}, u32[]{:S(2)}, u32[]{:S(2)}) collective-permute-start(f32[128]{0:T(128)S(1)} %add.169), channel_id=1, source_target_pairs={{0,4},{1,5},{2,6},{3,7},{4,0},{5,1},{6,2},{7,3},{8,12},{9,13},{10,... | collective-permute-start | bytes 1544 | tf_op jit(solution)/shard_map/ppermute | solution.py:23
  84.5 4.5 %collective-permute-start.8 = (f32[128]{0:T(128)S(1)}, f32[128]{0:T(128)S(1)}, u32[]{:S(2)}, u32[]{:S(2)}) collective-permute-start(f32[128]{0:T(128)S(1)} %add.176), channel_id=1, source_target_pairs={{0,4},{1,5},{2,6},{3,7},{4,0},{5,1},{6,2},{7,3},{8,12},{9,13},{10,... | collective-permute-start | bytes 1544 | tf_op jit(solution)/shard_map/ppermute | solution.py:23
  87.9 1.5 copy-start.24
  88.5 0.9 copy-start.27
  89.2 2.3 copy-start.32
  89.8 115.6 %copy-start.14 = (bf16[128,3,64]{2,0,1:T(8,128)(2,1)}, bf16[128,3,64]{2,0,1:T(8,128)(2,1)S(1)}, u32[]{:S(2)}) copy-start(bf16[128,3,64]{2,0,1:T(8,128)(2,1)S(1)} %get-tuple-element.371) | copy-start | bytes 147460
  89.8 115.6 %copy-start.15 = (bf16[128,3,64]{2,0,1:T(8,128)(2,1)}, bf16[128,3,64]{2,0,1:T(8,128)(2,1)S(1)}, u32[]{:S(2)}) copy-start(bf16[128,3,64]{2,0,1:T(8,128)(2,1)S(1)} %get-tuple-element.372) | copy-start | bytes 147460
  90.5 114.9 %copy-start.12 = (bf16[128,3,128]{2,0,1:T(8,128)(2,1)}, bf16[128,3,128]{2,0,1:T(8,128)(2,1)S(1)}, u32[]{:S(2)}) copy-start(bf16[128,3,128]{2,0,1:T(8,128)(2,1)S(1)} %maximum_convert_fusion) | copy-start | bytes 294916
  91.5 238.4 %all-gather.6.cloned.1.call-start = ((), (), s32[]{:S(2)}) async-start(), calls=%async_computation.4 | async-start | bytes 3342336 | tf_op jit(solution)/shard_map/all_gather | solution.py:43
  205.4 2.3 copy-start.33
  208.1 1.9 copy-start.2
  210.0 1.7 copy-start.34
  211.7 2.3 copy-start.33
  214.4 1.9 copy-start.2
  216.3 1.7 copy-start.34
  218.1 2.3 copy-start.33
  220.7 1.9 copy-start.2
  222.7 1.7 copy-start.34
  224.4 2.3 copy-start.33
  227.1 1.9 copy-start.2
  229.0 1.7 copy-start.34
  232.2 3.2 collective-permute-start.12
  235.3 4.3 %collective-permute-start.13 = (f32[128]{0:T(128)S(1)}, f32[128]{0:T(128)S(1)}, u32[]{:S(2)}, u32[]{:S(2)}) collective-permute-start(f32[128]{0:T(128)S(1)} %add.187), channel_id=1, source_target_pairs={{0,2},{1,3},{2,0},{3,1},{4,6},{5,7},{6,4},{7,5},{8,10},{9,11},{10,... | collective-permute-start | bytes 1544 | tf_op jit(solution)/shard_map/ppermute | solution.py:23
  239.6 4.3 %collective-permute-start.14 = (f32[128]{0:T(128)S(1)}, f32[128]{0:T(128)S(1)}, u32[]{:S(2)}, u32[]{:S(2)}) collective-permute-start(f32[128]{0:T(128)S(1)} %add.188), channel_id=1, source_target_pairs={{0,4},{1,5},{2,6},{3,7},{4,0},{5,1},{6,2},{7,3},{8,12},{9,13},{10,... | collective-permute-start | bytes 1544 | tf_op jit(solution)/shard_map/ppermute | solution.py:23
  245.9 84.0 %copy-start.13 = (bf16[128,3,128]{2,0,1:T(8,128)(2,1)S(1)}, bf16[128,3,128]{2,0,1:T(8,128)(2,1)}, u32[]{:S(2)}) copy-start(bf16[128,3,128]{2,0,1:T(8,128)(2,1)} %copy-done.12) | copy-start | bytes 294916
  291.8 40.3 %copy-start.11 = (bf16[128,384]{0,1:T(8,128)(2,1)S(1)}, bf16[128,384]{0,1:T(8,128)(2,1)}, u32[]{:S(2)}) copy-start(bf16[128,384]{0,1:T(8,128)(2,1)} %copy-done.10) | copy-start | bytes 294916
  329.9 2.4 copy-start
  329.9 2.4 copy-start.16
  332.1 1.6 copy-start.1
  333.7 3.6 copy-start.6
  333.7 3.6 copy-start.22
  333.7 3.6 copy-start.28
  333.7 18.2 %copy-start.4 = (bf16[128,384]{0,1:T(8,128)(2,1)S(1)}, bf16[128,384]{0,1:T(8,128)(2,1)}, u32[]{:S(2)}) copy-start(bf16[128,384]{0,1:T(8,128)(2,1)} %copy-done.3) | copy-start | bytes 294916
  333.7 18.2 %copy-start.20 = (f32[384]{0:T(512)S(1)}, f32[384]{0:T(512)}, u32[]{:S(2)}) copy-start(f32[384]{0:T(512)} %copy-done.19) | copy-start | bytes 4612
  333.7 18.2 %copy-start.25 = (f32[128]{0:T(128)S(1)}, f32[128]{0:T(128)}, u32[]{:S(2)}) copy-start(f32[128]{0:T(128)} %copy-done.24) | copy-start | bytes 1540
  341.0 16.0 %collective-permute-start.18 = (f32[128]{0:T(128)}, f32[128]{0:T(128)}, u32[]{:S(2)}, u32[]{:S(2)}) collective-permute-start(f32[128]{0:T(128)} %get-tuple-element.274), channel_id=1, source_target_pairs={{0,1},{1,0},{2,3},{3,2},{4,5},{5,4},{6,7},{7,6},{8,9},{9,8},{10,11... | collective-permute-start | bytes 1544 | tf_op jit(solution)/shard_map/ppermute | solution.py:23
  352.7 14.4 %collective-permute-start.15 = (f32[128]{0:T(128)}, f32[128]{0:T(128)}, u32[]{:S(2)}, u32[]{:S(2)}) collective-permute-start(f32[128]{0:T(128)} %get-tuple-element.272), channel_id=1, source_target_pairs={{0,1},{1,0},{2,3},{3,2},{4,5},{5,4},{6,7},{7,6},{8,9},{9,8},{10,11... | collective-permute-start | bytes 1544 | tf_op jit(solution)/shard_map/ppermute | solution.py:23
  358.2 12.3 %collective-permute-start.19 = (f32[128]{0:T(128)}, f32[128]{0:T(128)}, u32[]{:S(2)}, u32[]{:S(2)}) collective-permute-start(f32[128]{0:T(128)} %add.197), channel_id=1, source_target_pairs={{0,2},{1,3},{2,0},{3,1},{4,6},{5,7},{6,4},{7,5},{8,10},{9,11},{10,... | collective-permute-start | bytes 1544 | tf_op jit(solution)/shard_map/ppermute | solution.py:23
  362.9 22.4 %all-to-all-start = ((f32[16,1,6144]{2,1,0:T(1,128)}), f32[16,1,6144]{2,1,0:T(1,128)}, u32[]{:S(2)}, u32[]{:S(2)}) async-start(f32[16,1,6144]{2,1,0:T(1,128)} %broadcast_in_dim.18), calls=%async_computation | async-start | bytes 786432 | tf_op jit(solution)/shard_map/all_to_all | solution.py:48
  368.3 12.7 %collective-permute-start.16 = (f32[128]{0:T(128)}, f32[128]{0:T(128)}, u32[]{:S(2)}, u32[]{:S(2)}) collective-permute-start(f32[128]{0:T(128)} %add.193), channel_id=1, source_target_pairs={{0,2},{1,3},{2,0},{3,1},{4,6},{5,7},{6,4},{7,5},{8,10},{9,11},{10,... | collective-permute-start | bytes 1544 | tf_op jit(solution)/shard_map/ppermute | solution.py:23
  371.7 12.5 %copy-start.23 = (f32[384]{0:T(512)S(1)}, f32[384]{0:T(512)}, u32[]{:S(2)}) copy-start(f32[384]{0:T(512)} %copy-done.21) | copy-start | bytes 4612
  371.7 12.5 %copy-start.29 = (f32[128]{0:T(128)S(1)}, f32[128]{0:T(128)}, u32[]{:S(2)}) copy-start(f32[128]{0:T(128)} %copy-done.27) | copy-start | bytes 1540
  371.7 36.8 %copy-start.26 = (f32[128]{0:T(128)S(1)}, f32[128]{0:T(128)}, u32[]{:S(2)}) copy-start(f32[128]{0:T(128)} %copy-done.24) | copy-start | bytes 1540
  371.7 11.8 %collective-permute-start.20 = (f32[128]{0:T(128)}, f32[128]{0:T(128)}, u32[]{:S(2)}, u32[]{:S(2)}) collective-permute-start(f32[128]{0:T(128)} %add.198), channel_id=1, source_target_pairs={{0,4},{1,5},{2,6},{3,7},{4,0},{5,1},{6,2},{7,3},{8,12},{9,13},{10,... | collective-permute-start | bytes 1544 | tf_op jit(solution)/shard_map/ppermute | solution.py:23
  381.6 15.0 %collective-permute-start.17 = (f32[128]{0:T(128)S(1)}, f32[128]{0:T(128)S(1)}, u32[]{:S(2)}, u32[]{:S(2)}) collective-permute-start(f32[128]{0:T(128)S(1)} %add.194), channel_id=1, source_target_pairs={{0,4},{1,5},{2,6},{3,7},{4,0},{5,1},{6,2},{7,3},{8,12},{9,13},{10,... | collective-permute-start | bytes 1544 | tf_op jit(solution)/shard_map/ppermute | solution.py:23
  387.3 17.1 %all-to-all-start.1 = ((f32[32,1,96]{2,1,0:T(1,128)}), f32[32,1,96]{2,1,0:T(1,128)S(1)}, u32[]{:S(2)}, u32[]{:S(2)}) async-start(f32[32,1,96]{2,1,0:T(1,128)} %all_to_all.17), calls=%async_computation.1 | async-start | bytes 32768 | tf_op jit(solution)/shard_map/all_to_all | solution.py:73
  404.3 12.0 %all-to-all-start.2 = ((f32[32,1,96]{2,1,0:T(1,128)}), f32[32,1,96]{2,1,0:T(1,128)S(1)}, u32[]{:S(2)}, u32[]{:S(2)}) async-start(f32[32,1,96]{2,1,0:T(1,128)} %all_to_all.19), calls=%async_computation.2 | async-start | bytes 32768 | tf_op jit(solution)/shard_map/all_to_all | solution.py:73
  (6 other events, 4.6 us)
Sparse Core Ops, SparseCore 0:
  91.6 108.4 all-gather.3
  246.0 74.2 all-gather.5
where the time goes:
time: 426 us; the launch traced here: 424 us
  waiting for transfers between devices  125 us (29%)
  starting transfers between devices  84.4 us (20%)
  blocking collectives  72.7 us (17%)
  local copies, waits for them, and re-layouts  62.2 us (15%)
  matrix products  27.2 us (6%)
  other arithmetic  21.9 us (5%)
  between operations  16.6 us (4%)
  loops' own time  14.2 us (3%)
    all_gather x2, waiting for transfers between devices, sent_together(): lax.all_gather(both, axis, axis=dim, tiled=True)  107 us
    ppermute x21, starting transfers between devices, partner_2(): return lax.ppermute(value, axis, pairs)  66.7 us
    all_gather x1, blocking collectives, sent_together(): lax.all_gather(both, axis, axis=dim, tiled=True)  37.3 us
    all_gather x1, blocking collectives, gather_turned(): whole, at, outs = (lax.all_gather(both, axis, axis=0, tiled=True), 0, [])  35.4 us
    dynamic_slice x16, local copies, waits for them, and re-layouts, query_step(): lax.dynamic_slice_in_dim(gathered[1], block_id * tok_rows, tok_rows, 0)  14.9 us
    all_to_all x2, starting transfers between devices, sum_at_owner(): pieces = lax.all_to_all(split_up(x, dim, peers), axis, 0, 0, tiled=True)  13.4 us
    unnamed x82, local copies, waits for them, and re-layouts  12.7 us
    all_to_all x2, waiting for transfers between devices, sum_at_owner(): pieces = lax.all_to_all(split_up(x, dim, peers), axis, 0, 0, tiled=True)  12.1 us
  transfers between devices with their start and end apart: 26, of which 6 were waited for; matrix products, arithmetic and copies ran while one was open for 15% of the time, Pallas kernels for 0%

commit v1 on v0

v1 whole, which is shorter than its diff:
```python
import math

import jax
import jax.numpy as jnp
from jax import lax
from jax.experimental import pallas as pl
from jax.experimental.pallas import tpu as pltpu
from jax.sharding import PartitionSpec as P

MESH = pl.DeviceIdType.MESH
F32 = jnp.float32
BF16 = jnp.bfloat16

HD = 128
TOK = 128
STEPS = 1000
CHANNELS = 3072
HEADS_DEV = 3
N_CTX = 16
N_FSDP = 32
RANKS = 8
SAMPLES = 4
SLOTS = 8
ROWS = SLOTS * TOK
SEQ = 2 * ROWS
GSH = 96
CHUNK = 256
N_CHUNK = ROWS // CHUNK
KTILE = 512

eps_norm = 1e-06
loss_scale = 256.0
floor_term = 0.1
ROOT = math.sqrt(HD)
EXP2C = math.log2(math.e) / ROOT

LOC = ((0, 2, 9, 11, 4, 14), (5, 7, 14, 12, 9, 3))

NT = (((1,), (1,)), ((), ()))


def dot(a, b):
    return jnp.dot(a, b, preferred_element_type=F32)


def cols_to_rows(cols):
    lane = lax.broadcasted_iota(jnp.int32, (TOK, 128), 1)
    tile = jnp.zeros((TOK, 128), F32)
    for i, col in enumerate(cols):
        tile = jnp.where(lane == i, col, tile)
    return tile.T[0:8, :]


def rows_to_cols(rows):
    return jnp.concatenate([rows] * 16, axis=0).T


def kernel(
    so_ref,
    ti_ref,
    q_ref,
    k_ref,
    v_ref,
    qt_ref,
    kt_ref,
    vt_ref,
    qg_ref,
    kg_ref,
    dq_out,
    dk_out,
    dv_out,
    qgg_out,
    kgg_out,
    cosw,
    sinw,
    gsend,
    grecv,
    strecv,
    statc,
    gains,
    qs,
    ks,
    qq,
    kk,
    vv,
    vT,
    kT,
    s_buf,
    t_buf,
    e_buf,
    ds_buf,
    cn_buf,
    oT,
    gT,
    lrow,
    erecv,
    lev,
    resq,
    resk,
    resv,
    xsend,
    xrecv,
    retq,
    retk,
    retv,
    crecv,
    ggsend,
    ggrecv,
    ffrecv,
    g_ss,
    g_rs,
    st_ss,
    st_rs,
    v_ss,
    v_rs,
    q_ss,
    q_rs,
    k_ss,
    k_rs,
    fk_ss,
    fk_rs,
    fv_ss,
    fv_rs,
    e_ss,
    e_rs,
    r_ss,
    r_rs,
    x_ss,
    x_rs,
    c_ss,
    c_rs,
    gg_ss,
    gg_rs,
    ff_ss,
    ff_rs,
):
    c = lax.axis_index("ctx")
    f = lax.axis_index("fsdp")
    samp = f // 8
    rank = f % 8
    ylo = (f // 2) % 2
    core = f % 2
    base = f - core
    sib = base + (1 - core)
    half = c % 2
    slot = c // 2

    dests = []
    for h in range(HEADS_DEV):
        a, b = LOC[0][h], LOC[0][3 + h]
        d, e = LOC[1][h], LOC[1][3 + h]
        cd = a + core * (b - a) + ylo * (d - a) + core * ylo * (e - d - b + a)
        fd = base + half
        dests.append((cd, fd, jnp.logical_and(cd == c, fd == f)))

    act = 0
    jj = 0
    for j in range(6):
        hit = jnp.where(c == LOC[0][j] + ylo * (LOC[1][j] - LOC[0][j]), 1, 0)
        act = act + hit
        jj = jj + j * hit
    active = act == 1
    hcore = jj // 3
    hl = jj % 3
    src_f = base + hcore

    def source(t):
        cs = 2 * t + core
        return cs, src_f, jnp.logical_and(cs == c, src_f == f)

    def remote(src, dst, ss, rs, dev):
        return pltpu.make_async_remote_copy(
            src_ref=src, dst_ref=dst, send_sem=ss, recv_sem=rs, device_id=dev, device_id_type=MESH
        )

    def push(src, dst, ss, rs, dev, own):
        @pl.when(own)
        def _():
            pltpu.make_async_copy(src, dst, rs).start()

        @pl.when(jnp.logical_not(own))
        def _():
            remote(src, dst, ss, rs, dev).start()

    def sent(src, dst, ss, rs, dev, own):
        @pl.when(jnp.logical_not(own))
        def _():
            remote(src, dst, ss, rs, dev).wait_send()

    def arrived(dst, rs):
        pltpu.make_async_copy(dst, dst, rs).wait()

    barrier = pltpu.get_barrier_semaphore()
    for i in range(1, N_FSDP):
        pl.semaphore_signal(barrier, inc=1, device_id=(c, (f + i) % N_FSDP), device_id_type=MESH)
    own_heads = 0
    for cd, fd, own in dests:
        own_heads = own_heads + jnp.where(own, 1, 0)

        @pl.when(jnp.logical_not(own))
        def _(cd=cd, fd=fd):
            pl.semaphore_signal(barrier, inc=1, device_id=(cd, fd), device_id_type=MESH)

    @pl.when(active)
    def _():
        for t in range(SLOTS):
            cs, fs, own = source(t)

            @pl.when(jnp.logical_not(own))
            def _(cs=cs, fs=fs):
                pl.semaphore_signal(barrier, inc=1, device_id=(cs, fs), device_id_type=MESH)

    m_id = lax.broadcasted_iota(jnp.int32, (8, 128), 1) % 64
    freq = jnp.full((8, 128), 1.0, F32)
    for bit in range(6):
        factor = 10000.0 ** (-(2.0**bit) / 64.0)
        freq = freq * jnp.where((m_id // (2**bit)) % 2 == 1, factor, 1.0)
    row_id = lax.broadcasted_iota(jnp.int32, (TOK, 128), 0)
    place = (row_id + so_ref[0] * TOK).astype(F32)
    angle = place * freq[0:1, :]
    lane_id = lax.broadcasted_iota(jnp.int32, (TOK, 128), 1)
    cosw[...] = jnp.cos(angle)
    sin_t = jnp.sin(angle)
    sinw[...] = jnp.where(lane_id < 64, -sin_t, sin_t)

    qx = q_ref[...].astype(F32)
    kx = k_ref[...].astype(F32)
    qdx = qt_ref[...].astype(F32)
    kdx = kt_ref[...].astype(F32)

    def rsum(x):
        return jnp.sum(x, axis=1, keepdims=True)

    strecv[rank] = cols_to_rows([rsum(qx * qx), rsum(kx * kx), rsum(qx * qdx), rsum(kx * kdx)])
    gsend[...] = jnp.zeros((8, 128), F32)
    gsend[0:1, 0:GSH] = qg_ref[...]
    gsend[1:2, 0:GSH] = kg_ref[...]

    own_src = jnp.where(jnp.logical_and(half == core, hcore == core), 1, 0)
    pl.semaphore_wait(
        barrier, (N_FSDP - 1) + (HEADS_DEV - own_heads) + act * (SLOTS - own_src)
    )

    gain_copies = []
    for s in range(SAMPLES):
        fu = 8 * s + f // 4
        gain_copies.append(
            (gsend, grecv.at[f % 4], g_ss.at[s], g_rs.at[f % 4], (c, fu), fu == f)
        )
    for args in gain_copies:
        push(*args)
    stat_copies = []
    for i in range(1, RANKS):
        peer = samp * 8 + (rank + i) % 8
        stat_copies.append(
            remote(strecv.at[rank], strecv.at[rank], st_ss.at[i], st_rs.at[rank], (c, peer))
        )
    for copy in stat_copies:
        copy.start()
    val_copies = []
    for h, (cd, fd, own) in enumerate(dests):
        for n, ref in enumerate((v_ref, vt_ref)):
            val_copies.append(
                (
                    ref.at[:, h * HD : (h + 1) * HD],
                    vv.at[slot, :, n * HD : (n + 1) * HD],
                    v_ss.at[h, n],
                    v_rs.at[slot, n],
                    (cd, fd),
                    own,
                )
            )
    for args in val_copies:
        push(*args)

    for i in range(1, RANKS):
        peer = (rank + i) % 8
        arrived(strecv.at[peer], st_rs.at[peer])
    for i in range(4):
        arrived(grecv.at[i], g_rs.at[i])

    total = strecv[0]
    for i in range(1, RANKS):
        total = total + strecv[i]
    stat = rows_to_cols(total) / CHANNELS
    statc[...] = stat
    qr = lax.rsqrt(stat[:, 0:1] + eps_norm)
    kr = lax.rsqrt(stat[:, 1:2] + eps_norm)
    qc = stat[:, 2:3]
    kc = stat[:, 3:4]
    both = jnp.concatenate([grecv[i][:, 0:GSH] for i in range(4)], axis=1)
    gains[...] = both
    cos_w = cosw[...]
    sin_w = sinw[...]

    def turn(x, sign):
        return x * cos_w + sign * pltpu.roll(x, 64, 1) * sin_w

    def normed(x, dx, inv, cross, gain):
        y = x * inv * gain
        yt = (dx * inv - x * (inv * inv * inv) * cross) * gain
        return turn(y, 1.0).astype(BF16), turn(yt, 1.0).astype(BF16)

    qk_copies = []
    for h, (cd, fd, own) in enumerate(dests):
        cols = slice(h * HD, (h + 1) * HD)
        y, yt = normed(k_ref[:, cols].astype(F32), kt_ref[:, cols].astype(F32), kr, kc, both[1:2, cols])
        ks[h, :, 0:HD] = y
        ks[h, :, HD : 2 * HD] = yt
        args = (ks.at[h], kk.at[slot], k_ss.at[h], k_rs.at[slot], (cd, fd), own)
        push(*args)
        qk_copies.append(args)
    for h, (cd, fd, own) in enumerate(dests):
        cols = slice(h * HD, (h + 1) * HD)
        y, yt = normed(q_ref[:, cols].astype(F32), qt_ref[:, cols].astype(F32), qr, qc, both[0:1, cols])
        qs[h, :, 0:HD] = yt
        qs[h, :, HD : 2 * HD] = y
        args = (qs.at[h], qq.at[slot], q_ss.at[h], q_rs.at[slot], (cd, fd), own)
        push(*args)
        qk_copies.append(args)

    for args in gain_copies + val_copies + qk_copies:
        sent(*args)
    for copy in stat_copies:
        copy.wait_send()

    @pl.when(active)
    def _():
        for t in range(SLOTS):
            arrived(vv.at[t, :, 0:HD], v_rs.at[t, 0])
            arrived(vv.at[t, :, HD : 2 * HD], v_rs.at[t, 1])
            remote(vv.at[t], vv.at[SLOTS + t], fv_ss.at[t], fv_rs.at[t], (c, sib)).start()
        for t in range(SLOTS):
            arrived(kk.at[t], k_rs.at[t])
            remote(kk.at[t], kk.at[SLOTS + t], fk_ss.at[t], fk_rs.at[t], (c, sib)).start()
        for t in range(SLOTS):
            arrived(qq.at[t], q_rs.at[t])
        for t in range(SLOTS):
            remote(vv.at[t], vv.at[SLOTS + t], fv_ss.at[t], fv_rs.at[t], (c, sib)).wait()
            remote(kk.at[t], kk.at[SLOTS + t], fk_ss.at[t], fk_rs.at[t], (c, sib)).wait()
        for t in range(2 * SLOTS):
            rows = slice(t * TOK, (t + 1) * TOK)
            vT[:, rows] = vv[t].T
            kT[:, rows] = kk[t, :, 0:HD].T

        t_val = jnp.full((8, 128), ti_ref[samp], jnp.int32).astype(F32)
        t_ang = (0.5 * math.pi) * (t_val + 0.5) / STEPS
        sin_a = jnp.sin(t_ang)[0:1, :]
        cos_a = jnp.cos(t_ang)[0:1, :]
        c_out = jnp.concatenate([sin_a * cos_a] * 2, axis=1)
        c_tan = jnp.concatenate([cos_a * cos_a] * 2, axis=1)

        per = KTILE // TOK

        def forward(rc, carry):
            qb = qq[pl.ds(rc * 2, 2)].reshape(CHUNK, 2 * HD)
            peak = jnp.full((1, CHUNK), -jnp.inf, F32)
            for kt in range(SEQ // KTILE):
                kb = kk[kt * per : (kt + 1) * per, :, 0:HD].reshape(KTILE, HD)
                sc = lax.dot_general(kb, qb[:, HD : 2 * HD], NT, preferred_element_type=F32)
                s_buf[kt * KTILE : (kt + 1) * KTILE, :] = sc
                peak = jnp.maximum(peak, jnp.max(sc, axis=0, keepdims=True))
            shift = peak * EXP2C
            lsum = jnp.zeros((1, CHUNK), F32)
            tilt = jnp.zeros((1, CHUNK), F32)
            cols = pl.ds(pl.multiple_of(rc * CHUNK, CHUNK), CHUNK)
            for kt in range(SEQ // KTILE):
                rows = slice(kt * KTILE, (kt + 1) * KTILE)
                kb = kk[kt * per : (kt + 1) * per].reshape(KTILE, 2 * HD)
                up = lax.dot_general(kb, qb, NT, preferred_element_type=F32)
                ex = jnp.exp2(s_buf[rows, :] * EXP2C - shift)
                ti = ex * up
                lsum = lsum + jnp.sum(ex, axis=0, keepdims=True)
                tilt = tilt + jnp.sum(ti, axis=0, keepdims=True)
                e_buf[rows, cols] = ex.astype(BF16)
                t_buf[rows, :] = ti.astype(BF16)
            ov = dot(vT[...], e_buf[:, cols])
            tv = dot(vT[0:HD, :], t_buf[...])
            linv = 1.0 / lsum
            out = ov[0:HD, :] * linv
            out_t = (ov[HD : 2 * HD, :] + tv * (1.0 / ROOT)) * linv - (tilt * (1.0 / ROOT)) * linv * out
            oT[rc] = out
            gT[rc] = c_out * out + c_tan * out_t
            lrow[rc] = jnp.broadcast_to(linv, (8, CHUNK))
            return carry

        lax.fori_loop(0, N_CHUNK, forward, 0)

        energy = []
        for rc in range(N_CHUNK):
            g = gT[rc]
            e = jnp.sum(g * g, axis=0, keepdims=True)
            energy += [e[:, 0:128], e[:, 128:256]]
        mine = (rank // 2) * 6 + jj
        erecv[mine] = jnp.concatenate(energy, axis=0)
        for plane in range(4):
            for j in range(6):
                idx = plane * 6 + j
                fp = 8 * samp + plane * 2 + core

                @pl.when(mine != idx)
                def _(idx=idx, cp=LOC[plane % 2][j], fp=fp):
                    remote(
                        erecv.at[mine], erecv.at[mine], e_ss.at[idx], e_rs.at[mine], (cp, fp)
                    ).start()

        for idx in range(24):

            @pl.when(mine != idx)
            def _(idx=idx):
                arrived(erecv.at[idx], e_rs.at[idx])

        esum = erecv[0]
        for idx in range(1, 24):
            esum = esum + erecv[idx]
        scale = loss_scale / (jnp.sqrt(esum / CHANNELS) + floor_term)
        for rc in range(N_CHUNK):
            row = jnp.concatenate([scale[2 * rc : 2 * rc + 1], scale[2 * rc + 1 : 2 * rc + 2]], axis=1)
            lev[rc] = jnp.broadcast_to(row, (8, CHUNK))

        def back(rc, carry):
            cols = pl.ds(pl.multiple_of(rc * CHUNK, CHUNK), CHUNK)
            cot = (gT[rc] * lev[rc][0:1, :]).astype(BF16).astype(F32)
            cn = cot * (lrow[rc][0:1, :] * (1.0 / ROOT))
            cnT = cn.astype(BF16)
            drift = jnp.sum(cnT.astype(F32) * oT[rc], axis=0, keepdims=True)
            cn_buf[pl.ds(rc * 2, 2)] = cn.T.astype(BF16).reshape(2, TOK, HD)
            for kt in range(SEQ // KTILE):
                rows = slice(kt * KTILE, (kt + 1) * KTILE)
                vb = vv[kt * per : (kt + 1) * per, :, 0:HD].reshape(KTILE, HD)
                dp = dot(vb, cnT)
                ds_buf[rows, cols] = (e_buf[rows, cols].astype(F32) * (dp - drift)).astype(BF16)
            dqT = dot(kT[...], ds_buf[:, cols])
            resq[pl.ds(rc * 2, 2)] = dqT.T.astype(BF16).reshape(2, TOK, HD)
            for u in range(2):
                t = rc * 2 + u
                cs, fs, own = source(t)
                push(resq.at[t], retq.at[hl], r_ss.at[0, t], r_rs.at[0, hl], (cs, fs), own)
            return carry

        lax.fori_loop(0, N_CHUNK, back, 0)

        qn = qq[:, :, HD : 2 * HD].reshape(ROWS, HD)
        cn_all = cn_buf[...].reshape(ROWS, HD)
        xsend[0] = dot(ds_buf[ROWS:SEQ, :], qn).astype(BF16)
        xk = remote(xsend.at[0], xrecv.at[0], x_ss.at[0], x_rs.at[0], (c, sib))
        xk.start()
        xsend[1] = dot(e_buf[ROWS:SEQ, :], cn_all).astype(BF16)
        xv = remote(xsend.at[1], xrecv.at[1], x_ss.at[1], x_rs.at[1], (c, sib))
        xv.start()
        dk = dot(ds_buf[0:ROWS, :], qn)
        xk.wait_recv()
        resk[...] = (dk + xrecv[0].astype(F32)).astype(BF16).reshape(SLOTS, TOK, HD)
        for t in range(SLOTS):
            cs, fs, own = source(t)
            push(resk.at[t], retk.at[hl], r_ss.at[1, t], r_rs.at[1, hl], (cs, fs), own)
        dv = dot(e_buf[0:ROWS, :], cn_all)
        xv.wait_recv()
        resv[...] = ((dv + xrecv[1].astype(F32)) * ROOT).astype(BF16).reshape(SLOTS, TOK, HD)
        for t in range(SLOTS):
            cs, fs, own = source(t)
            push(resv.at[t], retv.at[hl], r_ss.at[2, t], r_rs.at[2, hl], (cs, fs), own)

        xk.wait_send()
        xv.wait_send()
        for t in range(SLOTS):
            cs, fs, own = source(t)
            sent(resq.at[t], retq.at[hl], r_ss.at[0, t], r_rs.at[0, hl], (cs, fs), own)
            sent(resk.at[t], retk.at[hl], r_ss.at[1, t], r_rs.at[1, hl], (cs, fs), own)
            sent(resv.at[t], retv.at[hl], r_ss.at[2, t], r_rs.at[2, hl], (cs, fs), own)
        for plane in range(4):
            for j in range(6):
                idx = plane * 6 + j
                fp = 8 * samp + plane * 2 + core

                @pl.when(mine != idx)
                def _(idx=idx, cp=LOC[plane % 2][j], fp=fp):
                    remote(
                        erecv.at[mine], erecv.at[mine], e_ss.at[idx], e_rs.at[mine], (cp, fp)
                    ).wait_send()

    def inverse_turn(ret):
        x = ret.astype(F32)
        return x * cosw[...] - pltpu.roll(x, 64, 1) * sinw[...]

    def inv_of(i):
        return lax.rsqrt(statc[:, i : i + 1] + eps_norm)

    crosses = []
    sums = []
    for i, (x_ref, ret, tensor) in enumerate(((q_ref, retq, 0), (k_ref, retk, 1))):
        inv = inv_of(i)
        part = jnp.zeros((TOK, HD), F32)
        rows = []
        for h in range(HEADS_DEV):
            cols = slice(h * HD, (h + 1) * HD)
            arrived(ret.at[h], r_rs.at[tensor, h])
            dyx = inverse_turn(ret[h]) * x_ref[:, cols].astype(F32)
            part = part + dyx * gains[i : i + 1, cols]
            rows.append(jnp.sum(dyx * inv, axis=0, keepdims=True))
        crosses.append(rsum(part))
        sums.append(jnp.concatenate(rows, axis=1))
    crecv[rank] = cols_to_rows(crosses)
    cross_copies = []
    for i in range(1, RANKS):
        peer = samp * 8 + (rank + i) % 8
        cross_copies.append(
            remote(crecv.at[rank], crecv.at[rank], c_ss.at[i], c_rs.at[rank], (c, peer))
        )
    for copy in cross_copies:
        copy.start()
    gg_copies = []
    ggsend[...] = jnp.zeros((4, 8, 128), F32)
    for i in range(4):
        for n in range(2):
            ggsend[i, n : n + 1, 0:GSH] = sums[n][:, i * GSH : (i + 1) * GSH]
        fo = 4 * rank + i
        gg_copies.append(
            (ggsend.at[i], ggrecv.at[samp], gg_ss.at[i], gg_rs.at[samp], (c, fo), fo == f)
        )
    for args in gg_copies:
        push(*args)

    for h in range(HEADS_DEV):
        arrived(retv.at[h], r_rs.at[2, h])
        dv_out[:, h * HD : (h + 1) * HD] = retv[h]

    for s in range(SAMPLES):
        arrived(ggrecv.at[s], gg_rs.at[s])
    ffrecv[c] = ggrecv[0] + ggrecv[1] + ggrecv[2] + ggrecv[3]
    ff_copies = []
    for i in range(1, N_CTX):
        ff_copies.append(
            remote(ffrecv.at[c], ffrecv.at[c], ff_ss.at[i], ff_rs.at[c], ((c + i) % N_CTX, f))
        )
    for copy in ff_copies:
        copy.start()

    for i in range(1, RANKS):
        peer = (rank + i) % 8
        arrived(crecv.at[peer], c_rs.at[peer])
    ctot = crecv[0]
    for i in range(1, RANKS):
        ctot = ctot + crecv[i]
    cmean = rows_to_cols(ctot) / CHANNELS
    for i, (x_ref, ret, out) in enumerate(((q_ref, retq, dq_out), (k_ref, retk, dk_out))):
        inv = inv_of(i)
        pull = inv * inv * inv * cmean[:, i : i + 1]
        for h in range(HEADS_DEV):
            cols = slice(h * HD, (h + 1) * HD)
            hh = inverse_turn(ret[h]) * gains[i : i + 1, cols]
            out[:, cols] = (inv * hh - x_ref[:, cols].astype(F32) * pull).astype(BF16)

    for i in range(1, N_CTX):
        peer = (c + i) % N_CTX
        arrived(ffrecv.at[peer], ff_rs.at[peer])
    ftot = ffrecv[0]
    for i in range(1, N_CTX):
        ftot = ftot + ffrecv[i]
    qgg_out[...] = ftot[0:1, 0:GSH]
    kgg_out[...] = ftot[1:2, 0:GSH]
    for copy in cross_copies + ff_copies:
        copy.wait_send()
    for args in gg_copies:
        sent(*args)


def per_device(
    queries,
    keys,
    values,
    query_tangent,
    key_tangent,
    value_tangent,
    query_gain,
    key_gain,
    time_index,
    shard_order,
):
    width = HEADS_DEV * HD
    vm = pl.BlockSpec(memory_space=pltpu.VMEM)
    sm = pl.BlockSpec(memory_space=pltpu.SMEM)
    dma = pltpu.SemaphoreType.DMA
    big = jax.ShapeDtypeStruct((TOK, width), BF16)
    small = jax.ShapeDtypeStruct((1, GSH), F32)
    scratch = [
        pltpu.VMEM((TOK, 128), F32),
        pltpu.VMEM((TOK, 128), F32),
        pltpu.VMEM((8, 128), F32),
        pltpu.VMEM((4, 8, 128), F32),
        pltpu.VMEM((8, 8, 128), F32),
        pltpu.VMEM((TOK, 128), F32),
        pltpu.VMEM((8, width), F32),
        pltpu.VMEM((3, TOK, 256), BF16),
        pltpu.VMEM((3, TOK, 256), BF16),
        pltpu.VMEM((SLOTS, TOK, 256), BF16),
        pltpu.VMEM((2 * SLOTS, TOK, 256), BF16),
        pltpu.VMEM((2 * SLOTS, TOK, 256), BF16),
        pltpu.VMEM((256, SEQ), BF16),
        pltpu.VMEM((128, SEQ), BF16),
        pltpu.VMEM((SEQ, CHUNK), F32),
        pltpu.VMEM((SEQ, CHUNK), BF16),
        pltpu.VMEM((SEQ, ROWS), BF16),
        pltpu.VMEM((SEQ, ROWS), BF16),
        pltpu.VMEM((SLOTS, TOK, HD), BF16),
        pltpu.VMEM((N_CHUNK, HD, CHUNK), F32),
        pltpu.VMEM((N_CHUNK, HD, CHUNK), F32),
        pltpu.VMEM((N_CHUNK, 8, CHUNK), F32),
        pltpu.VMEM((24, 8, 128), F32),
        pltpu.VMEM((N_CHUNK, 8, CHUNK), F32),
        pltpu.VMEM((SLOTS, TOK, HD), BF16),
        pltpu.VMEM((SLOTS, TOK, HD), BF16),
        pltpu.VMEM((SLOTS, TOK, HD), BF16),
        pltpu.VMEM((2, ROWS, HD), BF16),
        pltpu.VMEM((2, ROWS, HD), BF16),
        pltpu.VMEM((3, TOK, HD), BF16),
        pltpu.VMEM((3, TOK, HD), BF16),
        pltpu.VMEM((3, TOK, HD), BF16),
        pltpu.VMEM((8, 8, 128), F32),
        pltpu.VMEM((4, 8, 128), F32),
        pltpu.VMEM((4, 8, 128), F32),
        pltpu.VMEM((16, 8, 128), F32),
        dma((4,)),
        dma((4,)),
        dma((8,)),
        dma((8,)),
        dma((3, 2)),
        dma((8, 2)),
        dma((3,)),
        dma((8,)),
        dma((3,)),
        dma((8,)),
        dma((8,)),
        dma((8,)),
        dma((8,)),
        dma((8,)),
        dma((24,)),
        dma((24,)),
        dma((3, 8)),
        dma((3, 3)),
        dma((2,)),
        dma((2,)),
        dma((8,)),
        dma((8,)),
        dma((4,)),
        dma((4,)),
        dma((16,)),
        dma((16,)),
    ]
    outs = pl.pallas_call(
        kernel,
        out_shape=(big, big, big, small, small),
        in_specs=[sm, sm] + [vm] * 8,
        out_specs=(vm,) * 5,
        scratch_shapes=scratch,
        compiler_params=pltpu.CompilerParams(
            collective_id=0, has_side_effects=True, vmem_limit_bytes=48 * 1024 * 1024
        ),
        name="tangent_attention",
    )(
        shard_order,
        time_index,
        queries,
        keys,
        values,
        query_tangent,
        key_tangent,
        value_tangent,
        query_gain.reshape(1, GSH),
        key_gain.reshape(1, GSH),
    )
    return (outs[0], outs[1], outs[2], outs[3].reshape(GSH), outs[4].reshape(GSH))


def solution(mesh):
    placed = (
        P("ctx", "fsdp"),
        P("ctx", "fsdp"),
        P("ctx", "fsdp"),
        P("ctx", "fsdp"),
        P("ctx", "fsdp"),
        P("ctx", "fsdp"),
        P("fsdp"),
        P("fsdp"),
        P(),
        P("ctx"),
    )
    return jax.shard_map(
        per_device,
        mesh=mesh,
        in_specs=placed,
        out_specs=(P("ctx", "fsdp"), P("ctx", "fsdp"), P("ctx", "fsdp"), P("fsdp"), P("fsdp")),
        check_vma=False,
    )
```

time: 426 us -> 91.1 us (0.21)
  waiting for transfers between devices: 125 us -> 0 us
  starting transfers between devices: 84.4 us -> 0 us
  Pallas kernels: 0 us -> 80.5 us
  blocking collectives: 72.7 us -> 0 us
  local copies, waits for them, and re-layouts: 62.2 us -> 8.96 us
  matrix products: 27.2 us -> 0 us
  other arithmetic: 21.9 us -> 0 us
  between operations: 16.6 us -> 1.32 us
  loops' own time: 14.2 us -> 0 us
    all_gather x2 -> x0, waiting for transfers between devices: 107 us -> none  [sent_together(): lax.all_gather(both, axis, axis=dim, tiled=True)]
    pallas_call x0 -> x1, Pallas kernels: none -> 80.5 us  [per_device(): pl.pallas_call(kernel, out_shape=(big, big, big, small, small), in_specs=...]
    all_gather x2 -> x0, blocking collectives: 72.7 us -> none  [the longest x1 37.3 us: sent_together(): lax.all_gather(both, axis, axis=dim, tiled=True)]
    ppermute x21 -> x0, starting transfers between devices: 66.7 us -> none  [partner_2(): return lax.ppermute(value, axis, pairs)]
    dynamic_slice x46 -> x0, local copies, waits for them, and re-layouts: 35.7 us -> none  [the longest x16 14.9 us: query_step(): lax.dynamic_slice_in_dim(gathered[1], block_id * tok_rows, tok_rows, 0)]
    dot_general x60 -> x0, matrix products: 27.2 us -> none  [the longest x16 6.8 us: query_side(): jnp.einsum('thk,khd->thd', dscore, key_blk, preferred_element_type=jnp.fl...]
    all_to_all x3 -> x0, starting transfers between devices: 17.7 us -> none  [the longest x2 13.4 us: sum_at_owner(): pieces = lax.all_to_all(split_up(x, dim, peers), axis, 0, 0, tiled=True)]
    another operation x2 -> x0, loops' own time: 14.2 us -> none  [the longest x1 11.1 us: per_device(): lax.scan(query_step, zero_field, jnp.arange(cycle_size, dtype=jnp.int32))]
  transfers between devices with their start and end apart: 26 -> 0, of which waited for: 6 -> 0; matrix products, arithmetic and copies ran while one was open for 15% -> 0% of each run, Pallas kernels for 0% -> 0%
where the time goes in v1:
time: 91.1 us; the launch traced here: 90.7 us
  Pallas kernels  80.5 us (88%)
  local copies, waits for them, and re-layouts  8.96 us (10%)
  between operations  1.32 us (1%)
    pallas_call x1, Pallas kernels, per_device(): pl.pallas_call(kernel, out_shape=(big, big, big, small, small), in_specs=...  80.5 us
    unnamed x23, local copies, waits for them, and re-layouts  8.96 us

profile of v1, /device:TPU:1, one launch (start us, length us, event | category | flops | bytes accessed | tf_op | source)
XLA Modules:
  0.0 90.7 jit_solution(13712951467241137124)
XLA Ops:
  1.3 0.0 copy-start.6
  1.3 0.0 copy-start.7
  1.3 0.0 copy-start.8
  1.3 0.6 copy-done.6
  1.9 0.0 copy-done.7
  2.0 0.0 copy-done.8
  2.0 0.0 copy-start
  2.0 0.9 copy-done
  2.9 0.0 copy-start.1
  2.9 0.9 copy-done.1
  3.8 0.0 copy-start.2
  3.8 0.9 copy-done.2
  4.6 0.0 copy-start.3
  4.7 0.9 copy-done.3
  5.5 0.0 copy-start.4
  5.5 0.9 copy-done.4
  6.4 0.0 copy-start.5
  6.4 0.9 copy-done.5
  7.3 80.5 %tangent_attention.1 = (bf16[128,384]{1,0:T(8,128)(2,1)S(1)}, bf16[128,384]{1,0:T(8,128)(2,1)S(1)}, bf16[128,384]{1,0:T(8,128)(2,1)S(1)}, f32[1,96]{1,0:T(1,128)S(1)}, f32[1,96]{1,0:T(1,128)S(1)}) custom-call(s32[1]{0:T(128)S(6)} %copy.20.so_ref, s32[4]{0:T(128)S(1)} %copy-done.6, bf16[128,384]{1,0:T(8,128)(2,1)S(1)} %copy-done, ...), custom_call_target="tpu_custom_call" | custom-call | tf_op jit(solution)/shard_map/tangent_attention/pallas_call | solution.py:650
  87.8 0.6 copy.21
  88.4 0.6 copy.22
  89.1 0.6 copy.23
  89.7 0.5 copy.24
  90.2 0.5 copy.25
Async XLA Ops:
  1.3 0.7 copy-start.6
  1.3 0.7 copy-start.7
  1.3 0.7 copy-start.8
  2.0 0.9 copy-start
  2.9 0.9 copy-start.1
  3.8 0.9 copy-start.2
  4.6 0.9 copy-start.3
  5.5 0.9 copy-start.4
  6.4 0.9 copy-start.5

commit v2 on v1

--- a/solution.py
+++ b/solution.py
@@ -27,6 +27,7 @@
 CHUNK = 256
 N_CHUNK = ROWS // CHUNK
 KTILE = 512
+VMEM_LIMIT = 63 * 1024 * 1024
 
 eps_norm = 1e-06
 loss_scale = 256.0
@@ -58,14 +59,20 @@
 def kernel(
     so_ref,
     ti_ref,
-    q_ref,
-    k_ref,
-    v_ref,
-    qt_ref,
-    kt_ref,
-    vt_ref,
+    q_hbm,
+    k_hbm,
+    v_hbm,
+    qt_hbm,
+    kt_hbm,
+    vt_hbm,
     qg_ref,
     kg_ref,
+    dq_hbm,
+    dk_hbm,
+    dv_hbm,
+    qgg_hbm,
+    kgg_hbm,
+    loaded,
     dq_out,
     dk_out,
     dv_out,
@@ -94,7 +101,7 @@
     gT,
     lrow,
     erecv,
-    lev,
+    qn_buf,
     resq,
     resk,
     resv,
@@ -133,7 +140,10 @@
     gg_rs,
     ff_ss,
     ff_rs,
+    in_sem,
+    out_sem,
 ):
+    q_ref, k_ref, v_ref, qt_ref, kt_ref, vt_ref = (loaded.at[n] for n in range(6))
     c = lax.axis_index("ctx")
     f = lax.axis_index("fsdp")
     samp = f // 8
@@ -209,6 +219,13 @@
             @pl.when(jnp.logical_not(own))
             def _(cs=cs, fs=fs):
                 pl.semaphore_signal(barrier, inc=1, device_id=(cs, fs), device_id_type=MESH)
+
+    loads = [
+        pltpu.make_async_copy(src, loaded.at[n], in_sem.at[n])
+        for n, src in enumerate((q_hbm, k_hbm, v_hbm, qt_hbm, kt_hbm, vt_hbm))
+    ]
+    for load in loads:
+        load.start()
 
     m_id = lax.broadcasted_iota(jnp.int32, (8, 128), 1) % 64
     freq = jnp.full((8, 128), 1.0, F32)
@@ -223,6 +240,8 @@
     sin_t = jnp.sin(angle)
     sinw[...] = jnp.where(lane_id < 64, -sin_t, sin_t)
 
+    for load in loads:
+        load.wait()
     qx = q_ref[...].astype(F32)
     kx = k_ref[...].astype(F32)
     qdx = qt_ref[...].astype(F32)
@@ -404,6 +423,20 @@
                         erecv.at[mine], erecv.at[mine], e_ss.at[idx], e_rs.at[mine], (cp, fp)
                     ).start()
 
+        def back(rc, carry):
+            cols = pl.ds(pl.multiple_of(rc * CHUNK, CHUNK), CHUNK)
+            cnT = (gT[rc] * (lrow[rc][0:1, :] * (1.0 / ROOT))).astype(BF16)
+            drift = jnp.sum(cnT.astype(F32) * oT[rc], axis=0, keepdims=True)
+            for kt in range(SEQ // KTILE):
+                rows = slice(kt * KTILE, (kt + 1) * KTILE)
+                vb = vv[kt * per : (kt + 1) * per, :, 0:HD].reshape(KTILE, HD)
+                dp = dot(vb, cnT)
+                ds_buf[rows, cols] = (e_buf[rows, cols].astype(F32) * (dp - drift)).astype(BF16)
+            oT[rc] = dot(kT[...], ds_buf[:, cols])
+            return carry
+
+        lax.fori_loop(0, N_CHUNK, back, 0)
+
         for idx in range(24):
 
             @pl.when(mine != idx)
@@ -416,31 +449,19 @@
         scale = loss_scale / (jnp.sqrt(esum / CHANNELS) + floor_term)
         for rc in range(N_CHUNK):
             row = jnp.concatenate([scale[2 * rc : 2 * rc + 1], scale[2 * rc + 1 : 2 * rc + 2]], axis=1)
-            lev[rc] = jnp.broadcast_to(row, (8, CHUNK))
-
-        def back(rc, carry):
-            cols = pl.ds(pl.multiple_of(rc * CHUNK, CHUNK), CHUNK)
-            cot = (gT[rc] * lev[rc][0:1, :]).astype(BF16).astype(F32)
-            cn = cot * (lrow[rc][0:1, :] * (1.0 / ROOT))
-            cnT = cn.astype(BF16)
-            drift = jnp.sum(cnT.astype(F32) * oT[rc], axis=0, keepdims=True)
-            cn_buf[pl.ds(rc * 2, 2)] = cn.T.astype(BF16).reshape(2, TOK, HD)
-            for kt in range(SEQ // KTILE):
-                rows = slice(kt * KTILE, (kt + 1) * KTILE)
-                vb = vv[kt * per : (kt + 1) * per, :, 0:HD].reshape(KTILE, HD)
-                dp = dot(vb, cnT)
-                ds_buf[rows, cols] = (e_buf[rows, cols].astype(F32) * (dp - drift)).astype(BF16)
-            dqT = dot(kT[...], ds_buf[:, cols])
-            resq[pl.ds(rc * 2, 2)] = dqT.T.astype(BF16).reshape(2, TOK, HD)
-            for u in range(2):
-                t = rc * 2 + u
+            resq[2 * rc : 2 * rc + 2] = (oT[rc] * row).T.astype(BF16).reshape(2, TOK, HD)
+            cn = gT[rc] * (lrow[rc][0:1, :] * row * (1.0 / ROOT))
+            cn_buf[2 * rc : 2 * rc + 2] = cn.T.astype(BF16).reshape(2, TOK, HD)
+            for t in (2 * rc, 2 * rc + 1):
                 cs, fs, own = source(t)
                 push(resq.at[t], retq.at[hl], r_ss.at[0, t], r_rs.at[0, hl], (cs, fs), own)
-            return carry
-
-        lax.fori_loop(0, N_CHUNK, back, 0)
-
-        qn = qq[:, :, HD : 2 * HD].reshape(ROWS, HD)
+        scale_c = rows_to_cols(scale)
+        for t in range(SLOTS):
+            qn_buf[t * TOK : (t + 1) * TOK, :] = (
+                qq[t, :, HD : 2 * HD].astype(F32) * scale_c[:, t : t + 1]
+            ).astype(BF16)
+
+        qn = qn_buf[...]
         cn_all = cn_buf[...].reshape(ROWS, HD)
         xsend[0] = dot(ds_buf[ROWS:SEQ, :], qn).astype(BF16)
         xk = remote(xsend.at[0], xrecv.at[0], x_ss.at[0], x_rs.at[0], (c, sib))
@@ -524,6 +545,19 @@
     for h in range(HEADS_DEV):
         arrived(retv.at[h], r_rs.at[2, h])
         dv_out[:, h * HD : (h + 1) * HD] = retv[h]
+    stores = [
+        pltpu.make_async_copy(src, dst, out_sem.at[n])
+        for n, (src, dst) in enumerate(
+            (
+                (dq_out, dq_hbm),
+                (dk_out, dk_hbm),
+                (dv_out, dv_hbm),
+                (qgg_out, qgg_hbm),
+                (kgg_out, kgg_hbm),
+            )
+        )
+    ]
+    stores[2].start()
 
     for s in range(SAMPLES):
         arrived(ggrecv.at[s], gg_rs.at[s])
@@ -550,6 +584,7 @@
             cols = slice(h * HD, (h + 1) * HD)
             hh = inverse_turn(ret[h]) * gains[i : i + 1, cols]
             out[:, cols] = (inv * hh - x_ref[:, cols].astype(F32) * pull).astype(BF16)
+        stores[i].start()
 
     for i in range(1, N_CTX):
         peer = (c + i) % N_CTX
@@ -559,10 +594,27 @@
         ftot = ftot + ffrecv[i]
     qgg_out[...] = ftot[0:1, 0:GSH]
     kgg_out[...] = ftot[1:2, 0:GSH]
+    stores[3].start()
+    stores[4].start()
     for copy in cross_copies + ff_copies:
         copy.wait_send()
     for args in gg_copies:
         sent(*args)
+    for store in stores:
+        store.wait()
+
+
+def finish(*refs):
+    srcs, dsts, held, sem = refs[:5], refs[5:10], refs[10:15], refs[15]
+    reads = [pltpu.make_async_copy(srcs[n], held[n], sem.at[0, n]) for n in range(5)]
+    writes = [pltpu.make_async_copy(held[n], dsts[n], sem.at[1, n]) for n in range(5)]
+    for read in reads:
+        read.start()
+    for read, write in zip(reads, writes):
+        read.wait()
+        write.start()
+    for write in writes:
+        write.wait()
 
 
 def per_device(
@@ -579,11 +631,17 @@
 ):
     width = HEADS_DEV * HD
     vm = pl.BlockSpec(memory_space=pltpu.VMEM)
+    hbm = pl.BlockSpec(memory_space=pl.ANY)
     sm = pl.BlockSpec(memory_space=pltpu.SMEM)
     dma = pltpu.SemaphoreType.DMA
     big = jax.ShapeDtypeStruct((TOK, width), BF16)
-    small = jax.ShapeDtypeStruct((1, GSH), F32)
     scratch = [
+        pltpu.VMEM((6, TOK, width), BF16),
+        pltpu.VMEM((TOK, width), BF16),
+        pltpu.VMEM((TOK, width), BF16),
+        pltpu.VMEM((TOK, width), BF16),
+        pltpu.VMEM((1, GSH), F32),
+        pltpu.VMEM((1, GSH), F32),
         pltpu.VMEM((TOK, 128), F32),
         pltpu.VMEM((TOK, 128), F32),
         pltpu.VMEM((8, 128), F32),
@@ -607,7 +665,7 @@
         pltpu.VMEM((N_CHUNK, HD, CHUNK), F32),
         pltpu.VMEM((N_CHUNK, 8, CHUNK), F32),
         pltpu.VMEM((24, 8, 128), F32),
-        pltpu.VMEM((N_CHUNK, 8, CHUNK), F32),
+        pltpu.VMEM((ROWS, HD), BF16),
         pltpu.VMEM((SLOTS, TOK, HD), BF16),
         pltpu.VMEM((SLOTS, TOK, HD), BF16),
         pltpu.VMEM((SLOTS, TOK, HD), BF16),
@@ -646,15 +704,18 @@
         dma((4,)),
         dma((16,)),
         dma((16,)),
+        dma((6,)),
+        dma((5,)),
     ]
+    small = jax.ShapeDtypeStruct((1, GSH), F32)
     outs = pl.pallas_call(
         kernel,
         out_shape=(big, big, big, small, small),
-        in_specs=[sm, sm] + [vm] * 8,
-        out_specs=(vm,) * 5,
+        in_specs=[sm, sm] + [hbm] * 6 + [vm] * 2,
+        out_specs=(hbm,) * 5,
         scratch_shapes=scratch,
         compiler_params=pltpu.CompilerParams(
-            collective_id=0, has_side_effects=True, vmem_limit_bytes=48 * 1024 * 1024
+            collective_id=0, has_side_effects=True, vmem_limit_bytes=VMEM_LIMIT
         ),
         name="tangent_attention",
     )(
@@ -669,6 +730,15 @@
         query_gain.reshape(1, GSH),
         key_gain.reshape(1, GSH),
     )
+    outs = pl.pallas_call(
+        finish,
+        out_shape=(big, big, big, small, small),
+        in_specs=[hbm] * 5,
+        out_specs=(hbm,) * 5,
+        scratch_shapes=[pltpu.VMEM(a.shape, a.dtype) for a in outs] + [dma((2, 5))],
+        compiler_params=pltpu.CompilerParams(vmem_limit_bytes=VMEM_LIMIT),
+        name="store_results",
+    )(*outs)
     return (outs[0], outs[1], outs[2], outs[3].reshape(GSH), outs[4].reshape(GSH))
 
 

time: 91.1 us -> 82.1 us (0.901)
  local copies, waits for them, and re-layouts: 8.96 us -> 0 us
    unnamed x23 -> x0, local copies, waits for them, and re-layouts: 8.96 us -> none
    pallas_call x0 -> x1, Pallas kernels: none -> 1.72 us  [per_device(): pl.pallas_call(finish, out_shape=(big, big, big, small, small), in_specs=...]
    pallas_call x1, Pallas kernels: 80.5 us -> 78.9 us  [per_device(): pl.pallas_call(kernel, out_shape=(big, big, big, small, small), in_specs=...]
where the time goes in v2:
time: 82.1 us; the launch traced here: 81.9 us
  Pallas kernels  80.6 us (98%)
  between operations  1.29 us (2%)
    pallas_call x1, Pallas kernels, per_device(): pl.pallas_call(kernel, out_shape=(big, big, big, small, small), in_specs=...  78.9 us
    pallas_call x1, Pallas kernels, per_device(): pl.pallas_call(finish, out_shape=(big, big, big, small, small), in_specs=...  1.72 us

profile of v2, /device:TPU:1, one launch (start us, length us, event | category | flops | bytes accessed | tf_op | source)
XLA Modules:
  0.0 81.9 jit_solution(6487634719652436491)
XLA Ops:
  1.3 78.9 %tangent_attention.1 = (bf16[128,384]{1,0:T(8,128)(2,1)}, bf16[128,384]{1,0:T(8,128)(2,1)}, bf16[128,384]{1,0:T(8,128)(2,1)}, f32[1,96]{1,0:T(1,128)}, f32[1,96]{1,0:T(1,128)}) custom-call(s32[1]{0:T(128)S(6)} %copy.15.so_ref, s32[4]{0:T(128)} %ti_ref.1, bf16[128,384]{1,0:T(8,128)(2,1)} %q_hbm.1, bf16[128,384]{1,0:T(8,128)(2,1)} %k_hbm.1, ...), custom_call_target="tpu_custom_call" | custom-call | tf_op jit(solution)/shard_map/tangent_attention/pallas_call | solution.py:711
  80.2 1.7 %store_results.1 = (bf16[128,384]{1,0:T(8,128)(2,1)}, bf16[128,384]{1,0:T(8,128)(2,1)}, bf16[128,384]{1,0:T(8,128)(2,1)}, f32[1,96]{1,0:T(1,128)}, f32[1,96]{1,0:T(1,128)}) custom-call(bf16[128,384]{1,0:T(8,128)(2,1)} %get-tuple-element.15.refs_0_, bf16[128,384]{1,0:T(8,128)(2,1)} %get-tuple-element.16.refs_1_, bf16[128,384]{1,0:T(8,128)(2,1)} %get-tuple-element.17.refs_2_, ...), custom_call_target="tpu_custom_call" | custom-call | tf_op jit(solution)/shard_map/store_results/pallas_call | solution.py:733

commit v3 on v2

--- a/solution.py
+++ b/solution.py
@@ -27,6 +27,7 @@
 CHUNK = 256
 N_CHUNK = ROWS // CHUNK
 KTILE = 512
+EARLY = 3
 VMEM_LIMIT = 63 * 1024 * 1024
 
 eps_norm = 1e-06
@@ -78,15 +79,20 @@
     dv_out,
     qgg_out,
     kgg_out,
-    cosw,
-    sinw,
+    cr,
+    sr,
     gsend,
     grecv,
     strecv,
     statc,
-    gains,
-    qs,
-    ks,
+    msend,
+    mrecv,
+    mcol,
+    cosT,
+    sinT,
+    gain,
+    qraw,
+    kraw,
     qq,
     kk,
     vv,
@@ -97,11 +103,13 @@
     e_buf,
     ds_buf,
     cn_buf,
+    qn_buf,
     oT,
     gT,
+    dyq,
     lrow,
+    trow,
     erecv,
-    qn_buf,
     resq,
     resk,
     resv,
@@ -113,11 +121,13 @@
     crecv,
     ggsend,
     ggrecv,
-    ffrecv,
+    ggsum,
     g_ss,
     g_rs,
     st_ss,
     st_rs,
+    m_ss,
+    m_rs,
     v_ss,
     v_rs,
     q_ss,
@@ -138,8 +148,6 @@
     c_rs,
     gg_ss,
     gg_rs,
-    ff_ss,
-    ff_rs,
     in_sem,
     out_sem,
 ):
@@ -200,25 +208,47 @@
     def arrived(dst, rs):
         pltpu.make_async_copy(dst, dst, rs).wait()
 
+    own_rank, shard = f // 4, f % 4
+    head_rank = (rank // 4) * 4 + ylo * 2 + hcore
+    o_ylo, o_core = (own_rank // 2) % 2, own_rank % 2
+    feeds = []
+    for w in range(2):
+        hit = 0
+        for h in range(HEADS_DEV):
+            a, b = LOC[0][h], LOC[0][3 + h]
+            d, e = LOC[1][h], LOC[1][3 + h]
+            at = a + o_core * (b - a) + o_ylo * (d - a) + o_core * o_ylo * (e - d - b + a)
+            hit = hit + jnp.where(jnp.logical_and(at == c, shard == h + w), 1, 0)
+        feeds.append(hit)
+    fed = []
+    for s in range(SAMPLES):
+        for u in range(2):
+            fed.append((2 * s + own_rank // 4) * 4 + o_ylo * 2 + u)
+
     barrier = pltpu.get_barrier_semaphore()
-    for i in range(1, N_FSDP):
-        pl.semaphore_signal(barrier, inc=1, device_id=(c, (f + i) % N_FSDP), device_id_type=MESH)
-    own_heads = 0
-    for cd, fd, own in dests:
-        own_heads = own_heads + jnp.where(own, 1, 0)
-
+
+    def greet(dev, own):
         @pl.when(jnp.logical_not(own))
-        def _(cd=cd, fd=fd):
-            pl.semaphore_signal(barrier, inc=1, device_id=(cd, fd), device_id_type=MESH)
+        def _():
+            pl.semaphore_signal(barrier, inc=1, device_id=dev, device_id_type=MESH)
+
+    for i in range(1, RANKS):
+        pl.semaphore_signal(
+            barrier, inc=1, device_id=(c, samp * 8 + (rank + i) % 8), device_id_type=MESH
+        )
 
     @pl.when(active)
     def _():
         for t in range(SLOTS):
             cs, fs, own = source(t)
-
-            @pl.when(jnp.logical_not(own))
-            def _(cs=cs, fs=fs):
-                pl.semaphore_signal(barrier, inc=1, device_id=(cs, fs), device_id_type=MESH)
+            greet((cs, fs), own)
+        for w in range(2):
+            fo = 4 * head_rank + hl + w
+            greet((c, fo), fo == f)
+
+    for s in range(SAMPLES):
+        fu = 8 * s + own_rank
+        greet((c, fu), fu == f)
 
     loads = [
         pltpu.make_async_copy(src, loaded.at[n], in_sem.at[n])
@@ -233,12 +263,12 @@
         factor = 10000.0 ** (-(2.0**bit) / 64.0)
         freq = freq * jnp.where((m_id // (2**bit)) % 2 == 1, factor, 1.0)
     row_id = lax.broadcasted_iota(jnp.int32, (TOK, 128), 0)
-    place = (row_id + so_ref[0] * TOK).astype(F32)
-    angle = place * freq[0:1, :]
-    lane_id = lax.broadcasted_iota(jnp.int32, (TOK, 128), 1)
-    cosw[...] = jnp.cos(angle)
-    sin_t = jnp.sin(angle)
-    sinw[...] = jnp.where(lane_id < 64, -sin_t, sin_t)
+    angle = row_id.astype(F32) * freq[0:1, :]
+    cr[...] = jnp.cos(angle)
+    sr[...] = jnp.sin(angle)
+    gsend[...] = jnp.zeros((8, 128), F32)
+    gsend[0:1, 0:GSH] = qg_ref[...]
+    gsend[1:2, 0:GSH] = kg_ref[...]
 
     for load in loads:
         load.wait()
@@ -251,23 +281,19 @@
         return jnp.sum(x, axis=1, keepdims=True)
 
     strecv[rank] = cols_to_rows([rsum(qx * qx), rsum(kx * kx), rsum(qx * qdx), rsum(kx * kdx)])
-    gsend[...] = jnp.zeros((8, 128), F32)
-    gsend[0:1, 0:GSH] = qg_ref[...]
-    gsend[1:2, 0:GSH] = kg_ref[...]
-
-    own_src = jnp.where(jnp.logical_and(half == core, hcore == core), 1, 0)
+
+    own_heads = 0
+    for cd, fd, own in dests:
+        own_heads = own_heads + jnp.where(own, 1, 0)
+    own_shard = jnp.where(own_rank == rank, 1, 0)
+    own_fed = 0
+    for fd in fed:
+        own_fed = own_fed + jnp.where(fd == f, 1, 0)
+    feed = feeds[0] + feeds[1]
     pl.semaphore_wait(
-        barrier, (N_FSDP - 1) + (HEADS_DEV - own_heads) + act * (SLOTS - own_src)
+        barrier, (RANKS - 1) + (HEADS_DEV - own_heads) + (4 - own_shard) + feed * (8 - own_fed)
     )
 
-    gain_copies = []
-    for s in range(SAMPLES):
-        fu = 8 * s + f // 4
-        gain_copies.append(
-            (gsend, grecv.at[f % 4], g_ss.at[s], g_rs.at[f % 4], (c, fu), fu == f)
-        )
-    for args in gain_copies:
-        push(*args)
     stat_copies = []
     for i in range(1, RANKS):
         peer = samp * 8 + (rank + i) % 8
@@ -276,91 +302,100 @@
         )
     for copy in stat_copies:
         copy.start()
-    val_copies = []
-    for h, (cd, fd, own) in enumerate(dests):
-        for n, ref in enumerate((v_ref, vt_ref)):
-            val_copies.append(
-                (
-                    ref.at[:, h * HD : (h + 1) * HD],
-                    vv.at[slot, :, n * HD : (n + 1) * HD],
-                    v_ss.at[h, n],
-                    v_rs.at[slot, n],
-                    (cd, fd),
-                    own,
-                )
-            )
-    for args in val_copies:
+    gain_copies = []
+    for n, fd in enumerate(fed):
+        gain_copies.append((gsend, grecv.at[feeds[1]], g_ss.at[n], g_rs.at[feeds[1]], (c, fd), fd == f))
+
+    @pl.when(feed == 1)
+    def _():
+        for args in gain_copies:
+            push(*args)
+
+    tile_copies = []
+    for pair, dst, ss, rs in (
+        ((k_ref, kt_ref), lambda n: kraw.at[slot, n], k_ss, k_rs),
+        ((q_ref, qt_ref), lambda n: qraw.at[slot, n], q_ss, q_rs),
+        ((v_ref, vt_ref), lambda n: vv.at[slot, :, n * HD : (n + 1) * HD], v_ss, v_rs),
+    ):
+        for h, (cd, fd, own) in enumerate(dests):
+            for n, ref in enumerate(pair):
+                src = ref.at[:, h * HD : (h + 1) * HD]
+                tile_copies.append((src, dst(n), ss.at[h, n], rs.at[slot, n], (cd, fd), own))
+    for args in tile_copies:
         push(*args)
 
     for i in range(1, RANKS):
         peer = (rank + i) % 8
         arrived(strecv.at[peer], st_rs.at[peer])
-    for i in range(4):
-        arrived(grecv.at[i], g_rs.at[i])
-
     total = strecv[0]
     for i in range(1, RANKS):
         total = total + strecv[i]
-    stat = rows_to_cols(total) / CHANNELS
-    statc[...] = stat
-    qr = lax.rsqrt(stat[:, 0:1] + eps_norm)
-    kr = lax.rsqrt(stat[:, 1:2] + eps_norm)
-    qc = stat[:, 2:3]
-    kc = stat[:, 3:4]
-    both = jnp.concatenate([grecv[i][:, 0:GSH] for i in range(4)], axis=1)
-    gains[...] = both
-    cos_w = cosw[...]
-    sin_w = sinw[...]
-
-    def turn(x, sign):
-        return x * cos_w + sign * pltpu.roll(x, 64, 1) * sin_w
-
-    def normed(x, dx, inv, cross, gain):
-        y = x * inv * gain
-        yt = (dx * inv - x * (inv * inv * inv) * cross) * gain
-        return turn(y, 1.0).astype(BF16), turn(yt, 1.0).astype(BF16)
-
-    qk_copies = []
+    means = total / CHANNELS
+    start = jnp.full((8, 128), so_ref[0] * TOK, jnp.int32).astype(F32)
+    sub_id = lax.broadcasted_iota(jnp.int32, (8, 128), 0)
+    msend[...] = jnp.where(sub_id == 4, start, means)
+    meta_copies = []
     for h, (cd, fd, own) in enumerate(dests):
-        cols = slice(h * HD, (h + 1) * HD)
-        y, yt = normed(k_ref[:, cols].astype(F32), kt_ref[:, cols].astype(F32), kr, kc, both[1:2, cols])
-        ks[h, :, 0:HD] = y
-        ks[h, :, HD : 2 * HD] = yt
-        args = (ks.at[h], kk.at[slot], k_ss.at[h], k_rs.at[slot], (cd, fd), own)
+        meta_copies.append((msend, mrecv.at[slot], m_ss.at[h], m_rs.at[slot], (cd, fd), own))
+    for args in meta_copies:
         push(*args)
-        qk_copies.append(args)
-    for h, (cd, fd, own) in enumerate(dests):
-        cols = slice(h * HD, (h + 1) * HD)
-        y, yt = normed(q_ref[:, cols].astype(F32), qt_ref[:, cols].astype(F32), qr, qc, both[0:1, cols])
-        qs[h, :, 0:HD] = yt
-        qs[h, :, HD : 2 * HD] = y
-        args = (qs.at[h], qq.at[slot], q_ss.at[h], q_rs.at[slot], (cd, fd), own)
-        push(*args)
-        qk_copies.append(args)
-
-    for args in gain_copies + val_copies + qk_copies:
-        sent(*args)
-    for copy in stat_copies:
-        copy.wait_send()
+    statc[...] = rows_to_cols(means)
 
     @pl.when(active)
     def _():
         for t in range(SLOTS):
-            arrived(vv.at[t, :, 0:HD], v_rs.at[t, 0])
-            arrived(vv.at[t, :, HD : 2 * HD], v_rs.at[t, 1])
-            remote(vv.at[t], vv.at[SLOTS + t], fv_ss.at[t], fv_rs.at[t], (c, sib)).start()
-        for t in range(SLOTS):
-            arrived(kk.at[t], k_rs.at[t])
+            arrived(mrecv.at[t], m_rs.at[t])
+        for w in range(2):
+            arrived(grecv.at[w], g_rs.at[w])
+        lane8 = lax.broadcasted_iota(jnp.int32, (8, 128), 1)
+        gain[...] = jnp.where(
+            lane8 < GSH - 32 * hl,
+            pltpu.roll(grecv[0], (128 - 32 * hl) % 128, 1),
+            pltpu.roll(grecv[1], GSH - 32 * hl, 1),
+        )
+        starts = jnp.concatenate([mrecv[t][4:5, :] for t in range(SLOTS)], axis=0)
+        cb = jnp.cos(starts * freq)
+        sb = jnp.sin(starts * freq)
+        sign = jnp.where(lax.broadcasted_iota(jnp.int32, (TOK, 128), 1) < 64, -1.0, 1.0)
+
+        def turn(x, t):
+            return x * cosT[t] + pltpu.roll(x, 64, 1) * sinT[t]
+
+        def turn_back(x, t):
+            return x * cosT[t] - pltpu.roll(x, 64, 1) * sinT[t]
+
+        def inv_of(t, i):
+            return lax.rsqrt(mcol[t, :, i : i + 1] + eps_norm)
+
+        def normed(raw, t, i):
+            x = raw[t, 0].astype(F32)
+            dx = raw[t, 1].astype(F32)
+            inv = inv_of(t, i)
+            grow = gain[i : i + 1, :]
+            cross = mcol[t, :, i + 2 : i + 3]
+            y = x * inv * grow
+            yt = (dx * inv - x * (inv * inv * inv) * cross) * grow
+            return turn(y, t).astype(BF16), turn(yt, t).astype(BF16)
+
+        for t in range(SLOTS):
+            mcol[t] = rows_to_cols(mrecv[t])
+            cosT[t] = cb[t : t + 1] * cr[...] - sb[t : t + 1] * sr[...]
+            sinT[t] = sign * (sb[t : t + 1] * cr[...] + cb[t : t + 1] * sr[...])
+        for t in range(SLOTS):
+            for n in range(2):
+                arrived(kraw.at[t, n], k_rs.at[t, n])
+            y, yt = normed(kraw, t, 1)
+            kk[t, :, 0:HD] = y
+            kk[t, :, HD : 2 * HD] = yt
             remote(kk.at[t], kk.at[SLOTS + t], fk_ss.at[t], fk_rs.at[t], (c, sib)).start()
         for t in range(SLOTS):
-            arrived(qq.at[t], q_rs.at[t])
-        for t in range(SLOTS):
-            remote(vv.at[t], vv.at[SLOTS + t], fv_ss.at[t], fv_rs.at[t], (c, sib)).wait()
+            for n in range(2):
+                arrived(qraw.at[t, n], q_rs.at[t, n])
+            y, yt = normed(qraw, t, 0)
+            qq[t, :, 0:HD] = yt
+            qq[t, :, HD : 2 * HD] = y
+        for t in range(SLOTS):
             remote(kk.at[t], kk.at[SLOTS + t], fk_ss.at[t], fk_rs.at[t], (c, sib)).wait()
-        for t in range(2 * SLOTS):
-            rows = slice(t * TOK, (t + 1) * TOK)
-            vT[:, rows] = vv[t].T
-            kT[:, rows] = kk[t, :, 0:HD].T
 
         t_val = jnp.full((8, 128), ti_ref[samp], jnp.int32).astype(F32)
         t_ang = (0.5 * math.pi) * (t_val + 0.5) / STEPS
@@ -371,7 +406,7 @@
 
         per = KTILE // TOK
 
-        def forward(rc, carry):
+        def weigh(rc, carry):
             qb = qq[pl.ds(rc * 2, 2)].reshape(CHUNK, 2 * HD)
             peak = jnp.full((1, CHUNK), -jnp.inf, F32)
             for kt in range(SEQ // KTILE):
@@ -392,18 +427,37 @@
                 lsum = lsum + jnp.sum(ex, axis=0, keepdims=True)
                 tilt = tilt + jnp.sum(ti, axis=0, keepdims=True)
                 e_buf[rows, cols] = ex.astype(BF16)
-                t_buf[rows, :] = ti.astype(BF16)
+                t_buf[rows, cols] = ti.astype(BF16)
+            linv = 1.0 / lsum
+            lrow[rc] = jnp.broadcast_to(linv, (8, CHUNK))
+            trow[rc] = jnp.broadcast_to(tilt * (1.0 / ROOT) * linv, (8, CHUNK))
+            return carry
+
+        lax.fori_loop(0, EARLY, weigh, 0)
+        for t in range(SLOTS):
+            arrived(vv.at[t, :, 0:HD], v_rs.at[t, 0])
+            arrived(vv.at[t, :, HD : 2 * HD], v_rs.at[t, 1])
+            remote(vv.at[t], vv.at[SLOTS + t], fv_ss.at[t], fv_rs.at[t], (c, sib)).start()
+        lax.fori_loop(EARLY, N_CHUNK, weigh, 0)
+        for t in range(SLOTS):
+            vT[:, t * TOK : (t + 1) * TOK] = vv[t].T
+        for t in range(SLOTS):
+            rows = slice((SLOTS + t) * TOK, (SLOTS + t + 1) * TOK)
+            remote(vv.at[t], vv.at[SLOTS + t], fv_ss.at[t], fv_rs.at[t], (c, sib)).wait()
+            vT[:, rows] = vv[SLOTS + t].T
+
+        def combine(rc, carry):
+            cols = pl.ds(pl.multiple_of(rc * CHUNK, CHUNK), CHUNK)
             ov = dot(vT[...], e_buf[:, cols])
-            tv = dot(vT[0:HD, :], t_buf[...])
-            linv = 1.0 / lsum
+            tv = dot(vT[0:HD, :], t_buf[:, cols])
+            linv = lrow[rc][0:1, :]
             out = ov[0:HD, :] * linv
-            out_t = (ov[HD : 2 * HD, :] + tv * (1.0 / ROOT)) * linv - (tilt * (1.0 / ROOT)) * linv * out
+            out_t = (ov[HD : 2 * HD, :] + tv * (1.0 / ROOT)) * linv - trow[rc][0:1, :] * out
             oT[rc] = out
             gT[rc] = c_out * out + c_tan * out_t
-            lrow[rc] = jnp.broadcast_to(linv, (8, CHUNK))
             return carry
 
-        lax.fori_loop(0, N_CHUNK, forward, 0)
+        lax.fori_loop(0, N_CHUNK, combine, 0)
 
         energy = []
         for rc in range(N_CHUNK):
@@ -423,6 +477,9 @@
                         erecv.at[mine], erecv.at[mine], e_ss.at[idx], e_rs.at[mine], (cp, fp)
                     ).start()
 
+        for t in range(2 * SLOTS):
+            kT[:, t * TOK : (t + 1) * TOK] = kk[t, :, 0:HD].T
+
         def back(rc, carry):
             cols = pl.ds(pl.multiple_of(rc * CHUNK, CHUNK), CHUNK)
             cnT = (gT[rc] * (lrow[rc][0:1, :] * (1.0 / ROOT))).astype(BF16)
@@ -436,6 +493,8 @@
             return carry
 
         lax.fori_loop(0, N_CHUNK, back, 0)
+        for t in range(SLOTS):
+            dyq[t] = turn_back(oT[t // 2, :, (t % 2) * TOK : (t % 2 + 1) * TOK].T, t)
 
         for idx in range(24):
 
@@ -447,43 +506,84 @@
         for idx in range(1, 24):
             esum = esum + erecv[idx]
         scale = loss_scale / (jnp.sqrt(esum / CHANNELS) + floor_term)
-        for rc in range(N_CHUNK):
-            row = jnp.concatenate([scale[2 * rc : 2 * rc + 1], scale[2 * rc + 1 : 2 * rc + 2]], axis=1)
-            resq[2 * rc : 2 * rc + 2] = (oT[rc] * row).T.astype(BF16).reshape(2, TOK, HD)
-            cn = gT[rc] * (lrow[rc][0:1, :] * row * (1.0 / ROOT))
-            cn_buf[2 * rc : 2 * rc + 2] = cn.T.astype(BF16).reshape(2, TOK, HD)
-            for t in (2 * rc, 2 * rc + 1):
-                cs, fs, own = source(t)
-                push(resq.at[t], retq.at[hl], r_ss.at[0, t], r_rs.at[0, hl], (cs, fs), own)
         scale_c = rows_to_cols(scale)
         for t in range(SLOTS):
             qn_buf[t * TOK : (t + 1) * TOK, :] = (
                 qq[t, :, HD : 2 * HD].astype(F32) * scale_c[:, t : t + 1]
             ).astype(BF16)
-
         qn = qn_buf[...]
-        cn_all = cn_buf[...].reshape(ROWS, HD)
+
+        def finished(dy, t, i, raw):
+            inv = inv_of(t, i)
+            part = jnp.sum(dy * raw[t, 0].astype(F32) * inv, axis=0, keepdims=True)
+            return (dy * inv * gain[i : i + 1, :]).astype(BF16), part
+
+        ggq = jnp.zeros((1, HD), F32)
+        for t in range(SLOTS):
+            cs, fs, own = source(t)
+            resq[t], part = finished(dyq[t] * scale_c[:, t : t + 1], t, 0, qraw)
+            ggq = ggq + part
+            push(resq.at[t], retq.at[hl], r_ss.at[0, t], r_rs.at[0, hl], (cs, fs), own)
+
         xsend[0] = dot(ds_buf[ROWS:SEQ, :], qn).astype(BF16)
         xk = remote(xsend.at[0], xrecv.at[0], x_ss.at[0], x_rs.at[0], (c, sib))
         xk.start()
+        for rc in range(N_CHUNK):
+            row = jnp.concatenate([scale[2 * rc : 2 * rc + 1], scale[2 * rc + 1 : 2 * rc + 2]], axis=1)
+            cn = gT[rc] * (lrow[rc][0:1, :] * row * (1.0 / ROOT))
+            cn_buf[2 * rc : 2 * rc + 2] = cn.T.astype(BF16).reshape(2, TOK, HD)
+        cn_all = cn_buf[...].reshape(ROWS, HD)
         xsend[1] = dot(e_buf[ROWS:SEQ, :], cn_all).astype(BF16)
         xv = remote(xsend.at[1], xrecv.at[1], x_ss.at[1], x_rs.at[1], (c, sib))
         xv.start()
+
         dk = dot(ds_buf[0:ROWS, :], qn)
         xk.wait_recv()
-        resk[...] = (dk + xrecv[0].astype(F32)).astype(BF16).reshape(SLOTS, TOK, HD)
+        ggk = jnp.zeros((1, HD), F32)
         for t in range(SLOTS):
             cs, fs, own = source(t)
+            rows = slice(t * TOK, (t + 1) * TOK)
+            dkt = dk[rows, :] + xrecv[0, rows, :].astype(F32)
+            resk[t], part = finished(turn_back(dkt, t), t, 1, kraw)
+            ggk = ggk + part
             push(resk.at[t], retk.at[hl], r_ss.at[1, t], r_rs.at[1, hl], (cs, fs), own)
+        ggsend[...] = jnp.where(sub_id == 0, ggq, ggk)
+        member = samp * 2 + core
+        gg_copies = []
+        for i in range(N_CTX):
+            for w in range(2):
+                fo = 4 * head_rank + hl + w
+                own = fo == f if i == 0 else fo < 0
+                gg_copies.append(
+                    (
+                        ggsend,
+                        ggrecv.at[w, member],
+                        gg_ss.at[i, w],
+                        gg_rs.at[w, member],
+                        ((c + i) % N_CTX, fo),
+                        own,
+                    )
+                )
+        for n, args in enumerate(gg_copies):
+            if n < 2:
+                push(*args)
+            else:
+                remote(*args[:5]).start()
         dv = dot(e_buf[0:ROWS, :], cn_all)
         xv.wait_recv()
-        resv[...] = ((dv + xrecv[1].astype(F32)) * ROOT).astype(BF16).reshape(SLOTS, TOK, HD)
         for t in range(SLOTS):
             cs, fs, own = source(t)
+            rows = slice(t * TOK, (t + 1) * TOK)
+            resv[t] = ((dv[rows, :] + xrecv[1, rows, :].astype(F32)) * ROOT).astype(BF16)
             push(resv.at[t], retv.at[hl], r_ss.at[2, t], r_rs.at[2, hl], (cs, fs), own)
 
         xk.wait_send()
         xv.wait_send()
+        for n, args in enumerate(gg_copies):
+            if n < 2:
+                sent(*args)
+            else:
+                remote(*args[:5]).wait_send()
         for t in range(SLOTS):
             cs, fs, own = source(t)
             sent(resq.at[t], retq.at[hl], r_ss.at[0, t], r_rs.at[0, hl], (cs, fs), own)
@@ -500,27 +600,13 @@
                         erecv.at[mine], erecv.at[mine], e_ss.at[idx], e_rs.at[mine], (cp, fp)
                     ).wait_send()
 
-    def inverse_turn(ret):
-        x = ret.astype(F32)
-        return x * cosw[...] - pltpu.roll(x, 64, 1) * sinw[...]
-
-    def inv_of(i):
-        return lax.rsqrt(statc[:, i : i + 1] + eps_norm)
-
     crosses = []
-    sums = []
-    for i, (x_ref, ret, tensor) in enumerate(((q_ref, retq, 0), (k_ref, retk, 1))):
-        inv = inv_of(i)
+    for x_ref, ret, tensor in ((q_ref, retq, 0), (k_ref, retk, 1)):
         part = jnp.zeros((TOK, HD), F32)
-        rows = []
         for h in range(HEADS_DEV):
-            cols = slice(h * HD, (h + 1) * HD)
             arrived(ret.at[h], r_rs.at[tensor, h])
-            dyx = inverse_turn(ret[h]) * x_ref[:, cols].astype(F32)
-            part = part + dyx * gains[i : i + 1, cols]
-            rows.append(jnp.sum(dyx * inv, axis=0, keepdims=True))
+            part = part + ret[h].astype(F32) * x_ref[:, h * HD : (h + 1) * HD].astype(F32)
         crosses.append(rsum(part))
-        sums.append(jnp.concatenate(rows, axis=1))
     crecv[rank] = cols_to_rows(crosses)
     cross_copies = []
     for i in range(1, RANKS):
@@ -530,21 +616,7 @@
         )
     for copy in cross_copies:
         copy.start()
-    gg_copies = []
-    ggsend[...] = jnp.zeros((4, 8, 128), F32)
-    for i in range(4):
-        for n in range(2):
-            ggsend[i, n : n + 1, 0:GSH] = sums[n][:, i * GSH : (i + 1) * GSH]
-        fo = 4 * rank + i
-        gg_copies.append(
-            (ggsend.at[i], ggrecv.at[samp], gg_ss.at[i], gg_rs.at[samp], (c, fo), fo == f)
-        )
-    for args in gg_copies:
-        push(*args)
-
-    for h in range(HEADS_DEV):
-        arrived(retv.at[h], r_rs.at[2, h])
-        dv_out[:, h * HD : (h + 1) * HD] = retv[h]
+
     stores = [
         pltpu.make_async_copy(src, dst, out_sem.at[n])
         for n, (src, dst) in enumerate(
@@ -557,18 +629,10 @@
             )
         )
     ]
+    for h in range(HEADS_DEV):
+        arrived(retv.at[h], r_rs.at[2, h])
+        dv_out[:, h * HD : (h + 1) * HD] = retv[h]
     stores[2].start()
-
-    for s in range(SAMPLES):
-        arrived(ggrecv.at[s], gg_rs.at[s])
-    ffrecv[c] = ggrecv[0] + ggrecv[1] + ggrecv[2] + ggrecv[3]
-    ff_copies = []
-    for i in range(1, N_CTX):
-        ff_copies.append(
-            remote(ffrecv.at[c], ffrecv.at[c], ff_ss.at[i], ff_rs.at[c], ((c + i) % N_CTX, f))
-        )
-    for copy in ff_copies:
-        copy.start()
 
     for i in range(1, RANKS):
         peer = (rank + i) % 8
@@ -578,28 +642,45 @@
         ctot = ctot + crecv[i]
     cmean = rows_to_cols(ctot) / CHANNELS
     for i, (x_ref, ret, out) in enumerate(((q_ref, retq, dq_out), (k_ref, retk, dk_out))):
-        inv = inv_of(i)
-        pull = inv * inv * inv * cmean[:, i : i + 1]
+        pull = cmean[:, i : i + 1] / (statc[:, i : i + 1] + eps_norm)
         for h in range(HEADS_DEV):
             cols = slice(h * HD, (h + 1) * HD)
-            hh = inverse_turn(ret[h]) * gains[i : i + 1, cols]
-            out[:, cols] = (inv * hh - x_ref[:, cols].astype(F32) * pull).astype(BF16)
+            out[:, cols] = (ret[h].astype(F32) - x_ref[:, cols].astype(F32) * pull).astype(BF16)
         stores[i].start()
 
-    for i in range(1, N_CTX):
-        peer = (c + i) % N_CTX
-        arrived(ffrecv.at[peer], ff_rs.at[peer])
-    ftot = ffrecv[0]
-    for i in range(1, N_CTX):
-        ftot = ftot + ffrecv[i]
-    qgg_out[...] = ftot[0:1, 0:GSH]
-    kgg_out[...] = ftot[1:2, 0:GSH]
+    for w in range(2):
+        some = shard != 3 if w == 0 else shard != 0
+
+        @pl.when(some)
+        def _(w=w):
+            for n in range(8):
+                arrived(ggrecv.at[w, n], gg_rs.at[w, n])
+            acc = ggrecv[w, 0]
+            for n in range(1, 8):
+                acc = acc + ggrecv[w, n]
+            ggsum[w] = pltpu.roll(acc, 32 * shard, 1)
+
+        @pl.when(jnp.logical_not(some))
+        def _(w=w):
+            ggsum[w] = jnp.zeros((8, 128), F32)
+
+    glane = lax.broadcasted_iota(jnp.int32, (8, 128), 1)
+    gg = jnp.where(glane < 32 * shard, ggsum[1], ggsum[0])
+    qgg_out[...] = gg[0:1, 0:GSH]
+    kgg_out[...] = gg[1:2, 0:GSH]
     stores[3].start()
     stores[4].start()
-    for copy in cross_copies + ff_copies:
+
+    for copy in stat_copies + cross_copies:
         copy.wait_send()
-    for args in gg_copies:
+    for args in tile_copies + meta_copies:
         sent(*args)
+
+    @pl.when(feed == 1)
+    def _():
+        for args in gain_copies:
+            sent(*args)
+
     for store in stores:
         store.wait()
 
@@ -645,27 +726,34 @@
         pltpu.VMEM((TOK, 128), F32),
         pltpu.VMEM((TOK, 128), F32),
         pltpu.VMEM((8, 128), F32),
-        pltpu.VMEM((4, 8, 128), F32),
+        pltpu.VMEM((2, 8, 128), F32),
         pltpu.VMEM((8, 8, 128), F32),
         pltpu.VMEM((TOK, 128), F32),
-        pltpu.VMEM((8, width), F32),
-        pltpu.VMEM((3, TOK, 256), BF16),
-        pltpu.VMEM((3, TOK, 256), BF16),
+        pltpu.VMEM((8, 128), F32),
+        pltpu.VMEM((SLOTS, 8, 128), F32),
+        pltpu.VMEM((SLOTS, TOK, 128), F32),
+        pltpu.VMEM((SLOTS, TOK, 128), F32),
+        pltpu.VMEM((SLOTS, TOK, 128), F32),
+        pltpu.VMEM((8, 128), F32),
+        pltpu.VMEM((SLOTS, 2, TOK, HD), BF16),
+        pltpu.VMEM((SLOTS, 2, TOK, HD), BF16),
         pltpu.VMEM((SLOTS, TOK, 256), BF16),
         pltpu.VMEM((2 * SLOTS, TOK, 256), BF16),
         pltpu.VMEM((2 * SLOTS, TOK, 256), BF16),
         pltpu.VMEM((256, SEQ), BF16),
         pltpu.VMEM((128, SEQ), BF16),
         pltpu.VMEM((SEQ, CHUNK), F32),
-        pltpu.VMEM((SEQ, CHUNK), BF16),
+        pltpu.VMEM((SEQ, ROWS), BF16),
         pltpu.VMEM((SEQ, ROWS), BF16),
         pltpu.VMEM((SEQ, ROWS), BF16),
         pltpu.VMEM((SLOTS, TOK, HD), BF16),
+        pltpu.VMEM((ROWS, HD), BF16),
         pltpu.VMEM((N_CHUNK, HD, CHUNK), F32),
         pltpu.VMEM((N_CHUNK, HD, CHUNK), F32),
+        pltpu.VMEM((SLOTS, TOK, HD), F32),
+        pltpu.VMEM((N_CHUNK, 8, CHUNK), F32),
         pltpu.VMEM((N_CHUNK, 8, CHUNK), F32),
         pltpu.VMEM((24, 8, 128), F32),
-        pltpu.VMEM((ROWS, HD), BF16),
         pltpu.VMEM((SLOTS, TOK, HD), BF16),
         pltpu.VMEM((SLOTS, TOK, HD), BF16),
         pltpu.VMEM((SLOTS, TOK, HD), BF16),
@@ -675,19 +763,21 @@
         pltpu.VMEM((3, TOK, HD), BF16),
         pltpu.VMEM((3, TOK, HD), BF16),
         pltpu.VMEM((8, 8, 128), F32),
-        pltpu.VMEM((4, 8, 128), F32),
-        pltpu.VMEM((4, 8, 128), F32),
-        pltpu.VMEM((16, 8, 128), F32),
-        dma((4,)),
-        dma((4,)),
-        dma((8,)),
+        pltpu.VMEM((8, 128), F32),
+        pltpu.VMEM((2, 8, 8, 128), F32),
+        pltpu.VMEM((2, 8, 128), F32),
+        dma((8,)),
+        dma((2,)),
+        dma((8,)),
+        dma((8,)),
+        dma((3,)),
         dma((8,)),
         dma((3, 2)),
         dma((8, 2)),
-        dma((3,)),
-        dma((8,)),
-        dma((3,)),
-        dma((8,)),
+        dma((3, 2)),
+        dma((8, 2)),
+        dma((3, 2)),
+        dma((8, 2)),
         dma((8,)),
         dma((8,)),
         dma((8,)),
@@ -700,10 +790,8 @@
         dma((2,)),
         dma((8,)),
         dma((8,)),
-        dma((4,)),
-        dma((4,)),
-        dma((16,)),
-        dma((16,)),
+        dma((16, 2)),
+        dma((2, 8)),
         dma((6,)),
         dma((5,)),
     ]

time: 82.1 us -> 78.9 us (0.961)
  Pallas kernels: 80.6 us -> 77.4 us
    pallas_call x1, Pallas kernels: 78.9 us -> 75.6 us  [per_device(): pl.pallas_call(kernel, out_shape=(big, big, big, small, small), in_specs=...]
where the time goes in v3:
time: 78.9 us; the launch traced here: 78.6 us
  Pallas kernels  77.4 us (98%)
  between operations  1.29 us (2%)
    pallas_call x1, Pallas kernels, per_device(): pl.pallas_call(kernel, out_shape=(big, big, big, small, small), in_specs=...  75.6 us
    pallas_call x1, Pallas kernels, per_device(): pl.pallas_call(finish, out_shape=(big, big, big, small, small), in_specs=...  1.72 us

profile of v3, /device:TPU:1, one launch (start us, length us, event | category | flops | bytes accessed | tf_op | source)
XLA Modules:
  0.0 78.6 jit_solution(653464400725502363)
XLA Ops:
  1.3 75.6 %tangent_attention.1 = (bf16[128,384]{1,0:T(8,128)(2,1)}, bf16[128,384]{1,0:T(8,128)(2,1)}, bf16[128,384]{1,0:T(8,128)(2,1)}, f32[1,96]{1,0:T(1,128)}, f32[1,96]{1,0:T(1,128)}) custom-call(s32[1]{0:T(128)S(6)} %copy.15.so_ref, s32[4]{0:T(128)} %ti_ref.1, bf16[128,384]{1,0:T(8,128)(2,1)} %q_hbm.1, bf16[128,384]{1,0:T(8,128)(2,1)} %k_hbm.1, ...), custom_call_target="tpu_custom_call" | custom-call | tf_op jit(solution)/shard_map/tangent_attention/pallas_call | solution.py:799
  76.9 1.7 %store_results.1 = (bf16[128,384]{1,0:T(8,128)(2,1)}, bf16[128,384]{1,0:T(8,128)(2,1)}, bf16[128,384]{1,0:T(8,128)(2,1)}, f32[1,96]{1,0:T(1,128)}, f32[1,96]{1,0:T(1,128)}) custom-call(bf16[128,384]{1,0:T(8,128)(2,1)} %get-tuple-element.15.refs_0_, bf16[128,384]{1,0:T(8,128)(2,1)} %get-tuple-element.16.refs_1_, bf16[128,384]{1,0:T(8,128)(2,1)} %get-tuple-element.17.refs_2_, ...), custom_call_target="tpu_custom_call" | custom-call | tf_op jit(solution)/shard_map/store_results/pallas_call | solution.py:821

commit v4 on v3

--- a/solution.py
+++ b/solution.py
@@ -36,7 +36,7 @@
 ROOT = math.sqrt(HD)
 EXP2C = math.log2(math.e) / ROOT
 
-LOC = ((0, 2, 9, 11, 4, 14), (5, 7, 14, 12, 9, 3))
+LOC = ((1, 3, 10, 8, 5, 15), (6, 4, 15, 13, 10, 0))
 
 NT = (((1,), (1,)), ((), ()))
 
@@ -121,7 +121,10 @@
     crecv,
     ggsend,
     ggrecv,
-    ggsum,
+    ffsend,
+    ffrecv,
+    csend,
+    cpart,
     g_ss,
     g_rs,
     st_ss,
@@ -148,6 +151,10 @@
     c_rs,
     gg_ss,
     gg_rs,
+    ff_ss,
+    ff_rs,
+    p_ss,
+    p_rs,
     in_sem,
     out_sem,
 ):
@@ -246,10 +253,6 @@
             fo = 4 * head_rank + hl + w
             greet((c, fo), fo == f)
 
-    for s in range(SAMPLES):
-        fu = 8 * s + own_rank
-        greet((c, fu), fu == f)
-
     loads = [
         pltpu.make_async_copy(src, loaded.at[n], in_sem.at[n])
         for n, src in enumerate((q_hbm, k_hbm, v_hbm, qt_hbm, kt_hbm, vt_hbm))
@@ -285,13 +288,12 @@
     own_heads = 0
     for cd, fd, own in dests:
         own_heads = own_heads + jnp.where(own, 1, 0)
-    own_shard = jnp.where(own_rank == rank, 1, 0)
     own_fed = 0
     for fd in fed:
         own_fed = own_fed + jnp.where(fd == f, 1, 0)
     feed = feeds[0] + feeds[1]
     pl.semaphore_wait(
-        barrier, (RANKS - 1) + (HEADS_DEV - own_heads) + (4 - own_shard) + feed * (8 - own_fed)
+        barrier, (RANKS - 1) + (HEADS_DEV - own_heads) + feed * (8 - own_fed)
     )
 
     stat_copies = []
@@ -340,6 +342,13 @@
     for args in meta_copies:
         push(*args)
     statc[...] = rows_to_cols(means)
+
+    mine = (rank // 2) * 6 + jj
+    gg_copies = []
+    for w in range(2):
+        fo = 4 * head_rank + hl + w
+        dst = ggrecv.at[samp * 2 + core]
+        gg_copies.append((ggsend, dst, gg_ss.at[w], gg_rs.at[samp * 2 + core], (c, fo), fo == f))
 
     @pl.when(active)
     def _():
@@ -464,7 +473,6 @@
             g = gT[rc]
             e = jnp.sum(g * g, axis=0, keepdims=True)
             energy += [e[:, 0:128], e[:, 128:256]]
-        mine = (rank // 2) * 6 + jj
         erecv[mine] = jnp.concatenate(energy, axis=0)
         for plane in range(4):
             for j in range(6):
@@ -514,15 +522,19 @@
         qn = qn_buf[...]
 
         def finished(dy, t, i, raw):
-            inv = inv_of(t, i)
-            part = jnp.sum(dy * raw[t, 0].astype(F32) * inv, axis=0, keepdims=True)
-            return (dy * inv * gain[i : i + 1, :]).astype(BF16), part
+            x = raw[t, 0].astype(F32)
+            scaled = dy * inv_of(t, i)
+            grad = scaled * gain[i : i + 1, :]
+            part = jnp.sum(scaled * x, axis=0, keepdims=True)
+            return grad.astype(BF16), part, rsum(grad * x)
 
         ggq = jnp.zeros((1, HD), F32)
+        crosses = []
         for t in range(SLOTS):
             cs, fs, own = source(t)
-            resq[t], part = finished(dyq[t] * scale_c[:, t : t + 1], t, 0, qraw)
+            resq[t], part, cross = finished(dyq[t] * scale_c[:, t : t + 1], t, 0, qraw)
             ggq = ggq + part
+            crosses.append(cross)
             push(resq.at[t], retq.at[hl], r_ss.at[0, t], r_rs.at[0, hl], (cs, fs), own)
 
         xsend[0] = dot(ds_buf[ROWS:SEQ, :], qn).astype(BF16)
@@ -541,34 +553,28 @@
         xk.wait_recv()
         ggk = jnp.zeros((1, HD), F32)
         for t in range(SLOTS):
-            cs, fs, own = source(t)
             rows = slice(t * TOK, (t + 1) * TOK)
             dkt = dk[rows, :] + xrecv[0, rows, :].astype(F32)
-            resk[t], part = finished(turn_back(dkt, t), t, 1, kraw)
+            resk[t], part, cross = finished(turn_back(dkt, t), t, 1, kraw)
             ggk = ggk + part
+            crosses.append(cross)
+        lane_id = lax.broadcasted_iota(jnp.int32, (TOK, 128), 1)
+        ctile = jnp.zeros((TOK, 128), F32)
+        for n, cross in enumerate(crosses):
+            ctile = jnp.where(lane_id == n, cross, ctile)
+        ctile = ctile.T
+        for t in range(SLOTS):
+            cs, fs, own = source(t)
+            csend[t] = jnp.where(
+                sub_id == 0, ctile[t : t + 1, :], ctile[SLOTS + t : SLOTS + t + 1, :]
+            )
+            push(csend.at[t], cpart.at[hl], p_ss.at[t], p_rs.at[hl], (cs, fs), own)
+        for t in range(SLOTS):
+            cs, fs, own = source(t)
             push(resk.at[t], retk.at[hl], r_ss.at[1, t], r_rs.at[1, hl], (cs, fs), own)
         ggsend[...] = jnp.where(sub_id == 0, ggq, ggk)
-        member = samp * 2 + core
-        gg_copies = []
-        for i in range(N_CTX):
-            for w in range(2):
-                fo = 4 * head_rank + hl + w
-                own = fo == f if i == 0 else fo < 0
-                gg_copies.append(
-                    (
-                        ggsend,
-                        ggrecv.at[w, member],
-                        gg_ss.at[i, w],
-                        gg_rs.at[w, member],
-                        ((c + i) % N_CTX, fo),
-                        own,
-                    )
-                )
-        for n, args in enumerate(gg_copies):
-            if n < 2:
-                push(*args)
-            else:
-                remote(*args[:5]).start()
+        for args in gg_copies:
+            push(*args)
         dv = dot(e_buf[0:ROWS, :], cn_all)
         xv.wait_recv()
         for t in range(SLOTS):
@@ -577,37 +583,9 @@
             resv[t] = ((dv[rows, :] + xrecv[1, rows, :].astype(F32)) * ROOT).astype(BF16)
             push(resv.at[t], retv.at[hl], r_ss.at[2, t], r_rs.at[2, hl], (cs, fs), own)
 
-        xk.wait_send()
-        xv.wait_send()
-        for n, args in enumerate(gg_copies):
-            if n < 2:
-                sent(*args)
-            else:
-                remote(*args[:5]).wait_send()
-        for t in range(SLOTS):
-            cs, fs, own = source(t)
-            sent(resq.at[t], retq.at[hl], r_ss.at[0, t], r_rs.at[0, hl], (cs, fs), own)
-            sent(resk.at[t], retk.at[hl], r_ss.at[1, t], r_rs.at[1, hl], (cs, fs), own)
-            sent(resv.at[t], retv.at[hl], r_ss.at[2, t], r_rs.at[2, hl], (cs, fs), own)
-        for plane in range(4):
-            for j in range(6):
-                idx = plane * 6 + j
-                fp = 8 * samp + plane * 2 + core
-
-                @pl.when(mine != idx)
-                def _(idx=idx, cp=LOC[plane % 2][j], fp=fp):
-                    remote(
-                        erecv.at[mine], erecv.at[mine], e_ss.at[idx], e_rs.at[mine], (cp, fp)
-                    ).wait_send()
-
-    crosses = []
-    for x_ref, ret, tensor in ((q_ref, retq, 0), (k_ref, retk, 1)):
-        part = jnp.zeros((TOK, HD), F32)
-        for h in range(HEADS_DEV):
-            arrived(ret.at[h], r_rs.at[tensor, h])
-            part = part + ret[h].astype(F32) * x_ref[:, h * HD : (h + 1) * HD].astype(F32)
-        crosses.append(rsum(part))
-    crecv[rank] = cols_to_rows(crosses)
+    for h in range(HEADS_DEV):
+        arrived(cpart.at[h], p_rs.at[h])
+    crecv[rank] = cpart[0] + cpart[1] + cpart[2]
     cross_copies = []
     for i in range(1, RANKS):
         peer = samp * 8 + (rank + i) % 8
@@ -616,6 +594,30 @@
         )
     for copy in cross_copies:
         copy.start()
+
+    ff_copies = []
+    for i in range(N_CTX):
+        ff_copies.append(
+            (
+                ffsend,
+                ffrecv.at[feeds[1]],
+                ff_ss.at[i],
+                ff_rs.at[feeds[1]],
+                ((c + i) % N_CTX, f),
+            )
+        )
+
+    @pl.when(feed == 1)
+    def _():
+        for n in range(8):
+            arrived(ggrecv.at[n], gg_rs.at[n])
+        acc = ggrecv[0]
+        for n in range(1, 8):
+            acc = acc + ggrecv[n]
+        ffsend[...] = pltpu.roll(acc, 32 * shard, 1)
+        pltpu.make_async_copy(ffsend, ffrecv.at[feeds[1]], ff_rs.at[feeds[1]]).start()
+        for args in ff_copies[1:]:
+            remote(*args).start()
 
     stores = [
         pltpu.make_async_copy(src, dst, out_sem.at[n])
@@ -630,10 +632,8 @@
         )
     ]
     for h in range(HEADS_DEV):
-        arrived(retv.at[h], r_rs.at[2, h])
-        dv_out[:, h * HD : (h + 1) * HD] = retv[h]
-    stores[2].start()
-
+        arrived(retq.at[h], r_rs.at[0, h])
+        arrived(retk.at[h], r_rs.at[1, h])
     for i in range(1, RANKS):
         peer = (rank + i) % 8
         arrived(crecv.at[peer], c_rs.at[peer])
@@ -648,24 +648,24 @@
             out[:, cols] = (ret[h].astype(F32) - x_ref[:, cols].astype(F32) * pull).astype(BF16)
         stores[i].start()
 
+    for h in range(HEADS_DEV):
+        arrived(retv.at[h], r_rs.at[2, h])
+        dv_out[:, h * HD : (h + 1) * HD] = retv[h]
+    stores[2].start()
+
     for w in range(2):
         some = shard != 3 if w == 0 else shard != 0
 
         @pl.when(some)
         def _(w=w):
-            for n in range(8):
-                arrived(ggrecv.at[w, n], gg_rs.at[w, n])
-            acc = ggrecv[w, 0]
-            for n in range(1, 8):
-                acc = acc + ggrecv[w, n]
-            ggsum[w] = pltpu.roll(acc, 32 * shard, 1)
+            arrived(ffrecv.at[w], ff_rs.at[w])
 
         @pl.when(jnp.logical_not(some))
         def _(w=w):
-            ggsum[w] = jnp.zeros((8, 128), F32)
+            ffrecv[w] = jnp.zeros((8, 128), F32)
 
     glane = lax.broadcasted_iota(jnp.int32, (8, 128), 1)
-    gg = jnp.where(glane < 32 * shard, ggsum[1], ggsum[0])
+    gg = jnp.where(glane < 32 * shard, ffrecv[1], ffrecv[0])
     qgg_out[...] = gg[0:1, 0:GSH]
     kgg_out[...] = gg[1:2, 0:GSH]
     stores[3].start()
@@ -680,6 +680,31 @@
     def _():
         for args in gain_copies:
             sent(*args)
+        for args in ff_copies[1:]:
+            remote(*args).wait_send()
+
+    @pl.when(active)
+    def _():
+        for n in range(2):
+            remote(xsend.at[n], xrecv.at[n], x_ss.at[n], x_rs.at[n], (c, sib)).wait_send()
+        for args in gg_copies:
+            sent(*args)
+        for t in range(SLOTS):
+            cs, fs, own = source(t)
+            sent(csend.at[t], cpart.at[hl], p_ss.at[t], p_rs.at[hl], (cs, fs), own)
+            sent(resq.at[t], retq.at[hl], r_ss.at[0, t], r_rs.at[0, hl], (cs, fs), own)
+            sent(resk.at[t], retk.at[hl], r_ss.at[1, t], r_rs.at[1, hl], (cs, fs), own)
+            sent(resv.at[t], retv.at[hl], r_ss.at[2, t], r_rs.at[2, hl], (cs, fs), own)
+        for plane in range(4):
+            for j in range(6):
+                idx = plane * 6 + j
+                fp = 8 * samp + plane * 2 + core
+
+                @pl.when(mine != idx)
+                def _(idx=idx, cp=LOC[plane % 2][j], fp=fp):
+                    remote(
+                        erecv.at[mine], erecv.at[mine], e_ss.at[idx], e_rs.at[mine], (cp, fp)
+                    ).wait_send()
 
     for store in stores:
         store.wait()
@@ -764,8 +789,11 @@
         pltpu.VMEM((3, TOK, HD), BF16),
         pltpu.VMEM((8, 8, 128), F32),
         pltpu.VMEM((8, 128), F32),
-        pltpu.VMEM((2, 8, 8, 128), F32),
+        pltpu.VMEM((8, 8, 128), F32),
+        pltpu.VMEM((8, 128), F32),
         pltpu.VMEM((2, 8, 128), F32),
+        pltpu.VMEM((SLOTS, 8, 128), F32),
+        pltpu.VMEM((3, 8, 128), F32),
         dma((8,)),
         dma((2,)),
         dma((8,)),
@@ -790,8 +818,12 @@
         dma((2,)),
         dma((8,)),
         dma((8,)),
-        dma((16, 2)),
-        dma((2, 8)),
+        dma((2,)),
+        dma((8,)),
+        dma((16,)),
+        dma((2,)),
+        dma((8,)),
+        dma((3,)),
         dma((6,)),
         dma((5,)),
     ]

time: 78.9 us -> 77.9 us (0.987)
  the two profiles are of different devices: /device:TPU:1 before, /device:TPU:8 now
where the time goes in v4:
time: 77.9 us; the launch traced here: 77.7 us
  Pallas kernels  76.4 us (98%)
  between operations  1.29 us (2%)
    pallas_call x1, Pallas kernels, per_device(): pl.pallas_call(kernel, out_shape=(big, big, big, small, small), in_specs=...  74.7 us
    pallas_call x1, Pallas kernels, per_device(): pl.pallas_call(finish, out_shape=(big, big, big, small, small), in_specs=...  1.72 us

profile of v4, /device:TPU:8, one launch (start us, length us, event | category | flops | bytes accessed | tf_op | source)
XLA Modules:
  0.0 77.7 jit_solution(3455681767823310534)
XLA Ops:
  1.3 74.7 %tangent_attention.1 = (bf16[128,384]{1,0:T(8,128)(2,1)}, bf16[128,384]{1,0:T(8,128)(2,1)}, bf16[128,384]{1,0:T(8,128)(2,1)}, f32[1,96]{1,0:T(1,128)}, f32[1,96]{1,0:T(1,128)}) custom-call(s32[1]{0:T(128)S(6)} %copy.15.so_ref, s32[4]{0:T(128)} %ti_ref.1, bf16[128,384]{1,0:T(8,128)(2,1)} %q_hbm.1, bf16[128,384]{1,0:T(8,128)(2,1)} %k_hbm.1, ...), custom_call_target="tpu_custom_call" | custom-call | tf_op jit(solution)/shard_map/tangent_attention/pallas_call | solution.py:831
  76.0 1.7 %store_results.1 = (bf16[128,384]{1,0:T(8,128)(2,1)}, bf16[128,384]{1,0:T(8,128)(2,1)}, bf16[128,384]{1,0:T(8,128)(2,1)}, f32[1,96]{1,0:T(1,128)}, f32[1,96]{1,0:T(1,128)}) custom-call(bf16[128,384]{1,0:T(8,128)(2,1)} %get-tuple-element.15.refs_0_, bf16[128,384]{1,0:T(8,128)(2,1)} %get-tuple-element.16.refs_1_, bf16[128,384]{1,0:T(8,128)(2,1)} %get-tuple-element.17.refs_2_, ...), custom_call_target="tpu_custom_call" | custom-call | tf_op jit(solution)/shard_map/store_results/pallas_call | solution.py:853

commit v5 on v4

--- a/solution.py
+++ b/solution.py
@@ -323,7 +323,8 @@
             for n, ref in enumerate(pair):
                 src = ref.at[:, h * HD : (h + 1) * HD]
                 tile_copies.append((src, dst(n), ss.at[h, n], rs.at[slot, n], (cd, fd), own))
-    for args in tile_copies:
+    ahead = 4 * HEADS_DEV
+    for args in tile_copies[:ahead]:
         push(*args)
 
     for i in range(1, RANKS):
@@ -339,7 +340,7 @@
     meta_copies = []
     for h, (cd, fd, own) in enumerate(dests):
         meta_copies.append((msend, mrecv.at[slot], m_ss.at[h], m_rs.at[slot], (cd, fd), own))
-    for args in meta_copies:
+    for args in meta_copies + tile_copies[ahead:]:
         push(*args)
     statc[...] = rows_to_cols(means)
 
@@ -352,8 +353,6 @@
 
     @pl.when(active)
     def _():
-        for t in range(SLOTS):
-            arrived(mrecv.at[t], m_rs.at[t])
         for w in range(2):
             arrived(grecv.at[w], g_rs.at[w])
         lane8 = lax.broadcasted_iota(jnp.int32, (8, 128), 1)
@@ -362,9 +361,6 @@
             pltpu.roll(grecv[0], (128 - 32 * hl) % 128, 1),
             pltpu.roll(grecv[1], GSH - 32 * hl, 1),
         )
-        starts = jnp.concatenate([mrecv[t][4:5, :] for t in range(SLOTS)], axis=0)
-        cb = jnp.cos(starts * freq)
-        sb = jnp.sin(starts * freq)
         sign = jnp.where(lax.broadcasted_iota(jnp.int32, (TOK, 128), 1) < 64, -1.0, 1.0)
 
         def turn(x, t):
@@ -386,23 +382,34 @@
             yt = (dx * inv - x * (inv * inv * inv) * cross) * grow
             return turn(y, t).astype(BF16), turn(yt, t).astype(BF16)
 
-        for t in range(SLOTS):
+        def take_keys(t):
+            arrived(mrecv.at[t], m_rs.at[t])
+            at = mrecv[t][4:5, :] * freq
+            cb = jnp.cos(at)[0:1, :]
+            sb = jnp.sin(at)[0:1, :]
             mcol[t] = rows_to_cols(mrecv[t])
-            cosT[t] = cb[t : t + 1] * cr[...] - sb[t : t + 1] * sr[...]
-            sinT[t] = sign * (sb[t : t + 1] * cr[...] + cb[t : t + 1] * sr[...])
-        for t in range(SLOTS):
+            cosT[t] = cb * cr[...] - sb * sr[...]
+            sinT[t] = sign * (sb * cr[...] + cb * sr[...])
             for n in range(2):
                 arrived(kraw.at[t, n], k_rs.at[t, n])
             y, yt = normed(kraw, t, 1)
             kk[t, :, 0:HD] = y
             kk[t, :, HD : 2 * HD] = yt
             remote(kk.at[t], kk.at[SLOTS + t], fk_ss.at[t], fk_rs.at[t], (c, sib)).start()
-        for t in range(SLOTS):
+
+        def take_queries(t):
             for n in range(2):
                 arrived(qraw.at[t, n], q_rs.at[t, n])
             y, yt = normed(qraw, t, 0)
             qq[t, :, 0:HD] = yt
             qq[t, :, HD : 2 * HD] = y
+
+        for t in range(SLOTS - 1, 0, -1):
+            take_keys(t)
+        for t in range(SLOTS - 1, 0, -1):
+            take_queries(t)
+        take_keys(0)
+        take_queries(0)
         for t in range(SLOTS):
             remote(kk.at[t], kk.at[SLOTS + t], fk_ss.at[t], fk_rs.at[t], (c, sib)).wait()
 
@@ -558,6 +565,9 @@
             resk[t], part, cross = finished(turn_back(dkt, t), t, 1, kraw)
             ggk = ggk + part
             crosses.append(cross)
+        ggsend[...] = jnp.where(sub_id == 0, ggq, ggk)
+        for args in gg_copies:
+            push(*args)
         lane_id = lax.broadcasted_iota(jnp.int32, (TOK, 128), 1)
         ctile = jnp.zeros((TOK, 128), F32)
         for n, cross in enumerate(crosses):
@@ -572,9 +582,6 @@
         for t in range(SLOTS):
             cs, fs, own = source(t)
             push(resk.at[t], retk.at[hl], r_ss.at[1, t], r_rs.at[1, hl], (cs, fs), own)
-        ggsend[...] = jnp.where(sub_id == 0, ggq, ggk)
-        for args in gg_copies:
-            push(*args)
         dv = dot(e_buf[0:ROWS, :], cn_all)
         xv.wait_recv()
         for t in range(SLOTS):

time: 77.9 us -> 74.8 us (0.960)
  Pallas kernels: 76.4 us -> 73.3 us
    pallas_call x1, Pallas kernels: 74.7 us -> 71.6 us  [per_device(): pl.pallas_call(kernel, out_shape=(big, big, big, small, small), in_specs=...]
where the time goes in v5:
time: 74.8 us; the launch traced here: 74.6 us
  Pallas kernels  73.3 us (98%)
  between operations  1.29 us (2%)
    pallas_call x1, Pallas kernels, per_device(): pl.pallas_call(kernel, out_shape=(big, big, big, small, small), in_specs=...  71.6 us
    pallas_call x1, Pallas kernels, per_device(): pl.pallas_call(finish, out_shape=(big, big, big, small, small), in_specs=...  1.72 us

profile of v5, /device:TPU:8, one launch (start us, length us, event | category | flops | bytes accessed | tf_op | source)
XLA Modules:
  0.0 74.6 jit_solution(8827270972296704463)
XLA Ops:
  1.3 71.6 %tangent_attention.1 = (bf16[128,384]{1,0:T(8,128)(2,1)}, bf16[128,384]{1,0:T(8,128)(2,1)}, bf16[128,384]{1,0:T(8,128)(2,1)}, f32[1,96]{1,0:T(1,128)}, f32[1,96]{1,0:T(1,128)}) custom-call(s32[1]{0:T(128)S(6)} %copy.15.so_ref, s32[4]{0:T(128)} %ti_ref.1, bf16[128,384]{1,0:T(8,128)(2,1)} %q_hbm.1, bf16[128,384]{1,0:T(8,128)(2,1)} %k_hbm.1, ...), custom_call_target="tpu_custom_call" | custom-call | tf_op jit(solution)/shard_map/tangent_attention/pallas_call | solution.py:838
  72.9 1.7 %store_results.1 = (bf16[128,384]{1,0:T(8,128)(2,1)}, bf16[128,384]{1,0:T(8,128)(2,1)}, bf16[128,384]{1,0:T(8,128)(2,1)}, f32[1,96]{1,0:T(1,128)}, f32[1,96]{1,0:T(1,128)}) custom-call(bf16[128,384]{1,0:T(8,128)(2,1)} %get-tuple-element.15.refs_0_, bf16[128,384]{1,0:T(8,128)(2,1)} %get-tuple-element.16.refs_1_, bf16[128,384]{1,0:T(8,128)(2,1)} %get-tuple-element.17.refs_2_, ...), custom_call_target="tpu_custom_call" | custom-call | tf_op jit(solution)/shard_map/store_results/pallas_call | solution.py:860

commit v6 on v5

--- a/solution.py
+++ b/solution.py
@@ -590,6 +590,30 @@
             resv[t] = ((dv[rows, :] + xrecv[1, rows, :].astype(F32)) * ROOT).astype(BF16)
             push(resv.at[t], retv.at[hl], r_ss.at[2, t], r_rs.at[2, hl], (cs, fs), own)
 
+    ff_copies = []
+    for i in range(N_CTX):
+        ff_copies.append(
+            (
+                ffsend,
+                ffrecv.at[feeds[1]],
+                ff_ss.at[i],
+                ff_rs.at[feeds[1]],
+                ((c + i) % N_CTX, f),
+            )
+        )
+
+    @pl.when(feed == 1)
+    def _():
+        for n in range(8):
+            arrived(ggrecv.at[n], gg_rs.at[n])
+        acc = ggrecv[0]
+        for n in range(1, 8):
+            acc = acc + ggrecv[n]
+        ffsend[...] = pltpu.roll(acc, 32 * shard, 1)
+        pltpu.make_async_copy(ffsend, ffrecv.at[feeds[1]], ff_rs.at[feeds[1]]).start()
+        for args in ff_copies[1:]:
+            remote(*args).start()
+
     for h in range(HEADS_DEV):
         arrived(cpart.at[h], p_rs.at[h])
     crecv[rank] = cpart[0] + cpart[1] + cpart[2]
@@ -601,30 +625,6 @@
         )
     for copy in cross_copies:
         copy.start()
-
-    ff_copies = []
-    for i in range(N_CTX):
-        ff_copies.append(
-            (
-                ffsend,
-                ffrecv.at[feeds[1]],
-                ff_ss.at[i],
-                ff_rs.at[feeds[1]],
-                ((c + i) % N_CTX, f),
-            )
-        )
-
-    @pl.when(feed == 1)
-    def _():
-        for n in range(8):
-            arrived(ggrecv.at[n], gg_rs.at[n])
-        acc = ggrecv[0]
-        for n in range(1, 8):
-            acc = acc + ggrecv[n]
-        ffsend[...] = pltpu.roll(acc, 32 * shard, 1)
-        pltpu.make_async_copy(ffsend, ffrecv.at[feeds[1]], ff_rs.at[feeds[1]]).start()
-        for args in ff_copies[1:]:
-            remote(*args).start()
 
     stores = [
         pltpu.make_async_copy(src, dst, out_sem.at[n])

time: 74.8 us -> 74.9 us (level)
  no operation moved by 1% of the time
where the time goes in v6:
time: 74.9 us; the launch traced here: 74.6 us
  Pallas kernels  73.4 us (98%)
  between operations  1.29 us (2%)
    pallas_call x1, Pallas kernels, per_device(): pl.pallas_call(kernel, out_shape=(big, big, big, small, small), in_specs=...  71.6 us
    pallas_call x1, Pallas kernels, per_device(): pl.pallas_call(finish, out_shape=(big, big, big, small, small), in_specs=...  1.72 us

profile of v6, /device:TPU:8, one launch (start us, length us, event | category | flops | bytes accessed | tf_op | source)
XLA Modules:
  0.0 74.6 jit_solution(3189055923998105562)
XLA Ops:
  1.3 71.6 %tangent_attention.1 = (bf16[128,384]{1,0:T(8,128)(2,1)}, bf16[128,384]{1,0:T(8,128)(2,1)}, bf16[128,384]{1,0:T(8,128)(2,1)}, f32[1,96]{1,0:T(1,128)}, f32[1,96]{1,0:T(1,128)}) custom-call(s32[1]{0:T(128)S(6)} %copy.15.so_ref, s32[4]{0:T(128)} %ti_ref.1, bf16[128,384]{1,0:T(8,128)(2,1)} %q_hbm.1, bf16[128,384]{1,0:T(8,128)(2,1)} %k_hbm.1, ...), custom_call_target="tpu_custom_call" | custom-call | tf_op jit(solution)/shard_map/tangent_attention/pallas_call | solution.py:838
  72.9 1.7 %store_results.1 = (bf16[128,384]{1,0:T(8,128)(2,1)}, bf16[128,384]{1,0:T(8,128)(2,1)}, bf16[128,384]{1,0:T(8,128)(2,1)}, f32[1,96]{1,0:T(1,128)}, f32[1,96]{1,0:T(1,128)}) custom-call(bf16[128,384]{1,0:T(8,128)(2,1)} %get-tuple-element.15.refs_0_, bf16[128,384]{1,0:T(8,128)(2,1)} %get-tuple-element.16.refs_1_, bf16[128,384]{1,0:T(8,128)(2,1)} %get-tuple-element.17.refs_2_, ...), custom_call_target="tpu_custom_call" | custom-call | tf_op jit(solution)/shard_map/store_results/pallas_call | solution.py:860
